TPU v7x, 128 devices: a whole 4x4x4 slice. The times are simulated.
128 devices in a mesh: str: 16 (over z, y), int: 8 (over x, core).
Axes of the slice: x: 4, y: 4, z: 4, core: 2. Of those that a mesh axis runs over, the one named last changes fastest.
Arguments:
- ci: bfloat16 [192, 128, 2, 2048], P('str', None, None, 'int'), may hold values from -6 to 6
- slabs: bfloat16 [2, 2, 2048, 2048], P(None, None, None, 'int')
- sector: int32 [192], P('str'), may hold values from 0 to 1
- dest_dev: int32 [192, 1], P('str'), may hold values from 0 to 15; in each aligned block of 12 rows (0 to 11, 12 to 23, ...) at most 2 rows name the same one
- dest_slot: int32 [192], P('str'), may hold values from 0 to 11
- coef: bfloat16 [192, 2], P('str'), may hold values from -4 to 4
Outputs:
- sigma_vector: bfloat16 [192, 128, 2, 2048], P('str', None, None, 'int')
Inputs may be any that keep to these rules, and one draw needn't show every extreme that they name: `dest_dev`: among the 12 blocks of one str device at most 2 name the same value, and exactly 2 do on some device.
All inputs are finite; a program needn't handle non-finite values.
Results may differ from a plain program's by a relative error of at most 0.001.
Values may be sent and summed in bfloat16 or wider, within the bound.
No kernel may reach another device: no remote copies, remote signals or barrier semaphores. Data moves between devices by JAX's collectives and lax.ppermute only.
A program may use at most 192 MiB of HBM per device.

v0:
```python
import functools

import jax
import jax.numpy as jnp
from jax import lax
from jax.experimental import pallas as pl
from jax.experimental.pallas import tpu as pltpu
from jax.sharding import PartitionSpec as P

CAP = 2
CHUNKS = (32, 48, 48)
META = 16
LIMIT = 16 * 2**20


def turn(y):
    rows, cols = y.shape
    z = y.reshape(rows // 8, 8, cols)
    even = lax.broadcasted_iota(jnp.int32, z.shape, 1) % 2 == 0
    after = pltpu.roll(z, 7, 1)
    before = pltpu.roll(z, 1, 1)
    return jnp.where(even, -after, before).reshape(rows, cols)


def split_kernel(ci, out):
    out[...] = ci[...].reshape(out.shape)


def split(ci, r0, rc):
    nblk, rows, two, cols = ci.shape
    unit = 16
    return pl.pallas_call(
        split_kernel,
        grid=(rc // unit,),
        in_specs=[pl.BlockSpec((nblk, unit, two, cols), lambda i: (0, r0 // unit + i, 0, 0))],
        out_specs=pl.BlockSpec((nblk, two * unit, cols), lambda i: (0, i, 0)),
        out_shape=jax.ShapeDtypeStruct((nblk, two * rc, cols), ci.dtype),
        compiler_params=pltpu.CompilerParams(vmem_limit_bytes=LIMIT),
    )(ci)


def product_kernel(place, sector, slot, inner, coef, *refs):
    pieces, slab = refs[:8], refs[8]
    diag, send, acc, diags, code, sem = refs[9:]
    s, c = pl.program_id(0), pl.program_id(1)
    nblk, rows, cols = diag.shape
    total = None
    for j, piece in enumerate(pieces):
        left = piece[...].reshape(nblk * rows, cols)
        right = slab[0, 0, pl.ds(pl.multiple_of(place[j] * cols, cols), cols), :]
        part = jnp.dot(left, right, preferred_element_type=jnp.float32)
        total = part if total is None else total + part
    acc[s, c] = total.reshape(nblk, rows, cols)

    @pl.when((s == 1) & (c == 1))
    def _():
        finish(sector, slot, inner, coef, acc, diags, code, diag, send, sem)


def finish(sector, slot, inner, coef, acc, diags, code, diag, send, sem):
    nblk, rows, cols = diag.shape
    line = lax.broadcasted_iota(jnp.int32, (META, cols), 0)
    half = line // (META // CAP)
    first_part = (line % (META // CAP)) < META // (2 * CAP)
    for dev in range(send.shape[0]):
        code[dev, CAP * rows :, :] = jnp.zeros((META, cols), jnp.int16)

    def block(b, carry):
        mine = sector[b]
        diags[b] = acc[mine, 0, b] + turn(acc[mine, 1, b])
        pltpu.make_async_copy(diags.at[b], diag.at[b], sem.at[0]).start()
        cr = coef[b, 0]
        ci = coef[b, 1]
        p = acc[1 - mine, 0, b]
        q = acc[1 - mine, 1, b]
        partner = (cr * p - ci * q) + turn(cr * q + ci * p)
        top = jnp.max(jnp.abs(partner), axis=0, keepdims=True)
        level = jnp.ceil(jnp.log2(jnp.maximum(top, 1.2e-38)) * 256.0) + 1.0
        level = jnp.clip(level, -32256.0, 32766.0)
        unit = jnp.exp2(level * (1.0 / 256.0))
        value = jnp.round(jnp.clip(partner * (1.0 / unit), -1.0, 1.0) * 32767.0)
        dev = slot[b] // CAP
        cap = slot[b] % CAP
        first = pl.multiple_of(cap * rows, 16)
        code[dev, pl.ds(first, rows), :] = value.astype(jnp.int32).astype(jnp.int16)
        old = code[dev, pl.ds(CAP * rows, META), :].astype(jnp.int32)
        new = jnp.where(first_part, level.astype(jnp.int32), inner[b] + 1)
        code[dev, pl.ds(CAP * rows, META), :] = jnp.where(half == cap, new, old).astype(jnp.int16)
        return carry

    lax.fori_loop(0, nblk, block, 0)
    copy = pltpu.make_async_copy(code, send, sem.at[1])
    copy.start()
    pltpu.make_async_copy(diags, diag, sem.at[0]).wait()
    copy.wait()


def product(pieces, slabs, place, sector, slot, inner, coef, nstr):
    nblk, rows, cols = pieces[0].shape
    vmem = pl.BlockSpec(memory_space=pltpu.VMEM)
    hbm = pl.BlockSpec(memory_space=pltpu.HBM)
    shape = (nstr, CAP * rows + META, cols)
    grid = pltpu.PrefetchScalarGridSpec(
        num_scalar_prefetch=5,
        grid=(2, 2),
        in_specs=[vmem] * 8 + [pl.BlockSpec((1, 1, slabs.shape[2], cols), lambda s, c, *_: (s, c, 0, 0))],
        out_specs=[hbm, hbm],
        scratch_shapes=[
            pltpu.VMEM((2, 2, nblk, rows, cols), jnp.float32),
            pltpu.VMEM((nblk, rows, cols), jnp.float32),
            pltpu.VMEM(shape, jnp.int16),
            pltpu.SemaphoreType.DMA((2,)),
        ],
    )
    return pl.pallas_call(
        product_kernel,
        grid_spec=grid,
        out_shape=[pltpu.HBM((nblk, rows, cols), jnp.float32), pltpu.HBM(shape, jnp.int16)],
        compiler_params=pltpu.CompilerParams(vmem_limit_bytes=LIMIT),
        cost_estimate=pl.CostEstimate(
            flops=2 * nblk * rows * cols * 8 * 4 * cols, bytes_accessed=14 * 2**20, transcendentals=0
        ),
    )(place, sector, slot, inner, coef, *pieces, slabs)


def add_kernel(r0, diag, recv, *refs):
    out, acc, done, sem = refs[-4:]
    nblk, rows, cols = diag.shape
    load = pltpu.make_async_copy(diag, acc, sem)
    load.start()
    load.wait()
    for dev in range(recv.shape[0]):
        meta = recv[dev, CAP * rows :, :].astype(jnp.int32)
        for cap in range(CAP):
            at = cap * (META // CAP)
            b = meta[at + META // (2 * CAP), 0] - 1

            @pl.when(b >= 0)
            def _():
                unit = jnp.exp2(meta[at : at + 1].astype(jnp.float32) * (1.0 / 256.0)) * (1.0 / 32767.0)
                code = recv[dev, cap * rows : (cap + 1) * rows, :].astype(jnp.int32).astype(jnp.float32)
                acc[b] += code * unit

    done[...] = acc[...].astype(done.dtype).reshape(done.shape)
    copy = pltpu.make_async_copy(done, out.at[:, pl.ds(r0, rows // 2)], sem)
    copy.start()
    copy.wait()


def add(diag, recv, r0, full, out):
    nblk, rows, cols = diag.shape
    rest = [] if out is None else [out]
    vmem = pl.BlockSpec(memory_space=pltpu.VMEM)
    hbm = pl.BlockSpec(memory_space=pltpu.HBM)
    return pl.pallas_call(
        functools.partial(add_kernel, r0),
        in_specs=[hbm, vmem] + [hbm] * len(rest),
        out_specs=hbm,
        scratch_shapes=[
            pltpu.VMEM(diag.shape, jnp.float32),
            pltpu.VMEM((nblk, rows // 2, 2, cols), jnp.bfloat16),
            pltpu.SemaphoreType.DMA,
        ],
        out_shape=pltpu.HBM(full.shape, full.dtype),
        input_output_aliases={2: 0} if rest else {},
        compiler_params=pltpu.CompilerParams(vmem_limit_bytes=LIMIT),
    )(pltpu.with_memory_space_constraint(diag, pltpu.HBM), recv, *rest)


def body(ci, slabs, sector, dest_dev, dest_slot, coef):
    nblk, rows, two, ncol = ci.shape
    nstr = lax.axis_size("str")
    nint = lax.axis_size("int")
    nx = nint // 2
    here = lax.axis_index("int")
    x = here // 2
    core = here % 2

    def ipos(a, c):
        return (a % nx) * 2 + c

    def way(c):
        return 1 - 2 * c

    pairs = [(a, c) for a in range(nx) for c in range(2)]
    ahead = [(ipos(a, c), ipos(a + way(c), c)) for a, c in pairs]
    back = [(ipos(a, c), ipos(a - way(c), c)) for a, c in pairs]
    swap = [(ipos(a, c), ipos(a, 1 - c)) for a, c in pairs]

    d = way(core)
    place = jnp.stack(
        [
            ipos(x, core), ipos(x - d, core), ipos(x + d, core), ipos(x + 2, core),
            ipos(x, 1 - core), ipos(x + d, 1 - core), ipos(x - d, 1 - core), ipos(x + 2, 1 - core),
        ]
    ).astype(jnp.int32)

    target = dest_dev[:, 0]
    order = jnp.arange(nblk, dtype=jnp.int32)
    same = (target[:, None] == target[None, :]) & (order[:, None] > order[None, :])
    slot = target * CAP + jnp.sum(same.astype(jnp.int32), axis=1)
    cwt = coef.astype(jnp.float32)

    def move(v, perm):
        return lax.ppermute(v, "int", perm)

    starts = [sum(CHUNKS[:i]) for i in range(len(CHUNKS))]
    n = len(CHUNKS)
    own = [split(ci, starts[i], CHUNKS[i]) for i in range(n)]
    held = pltpu.with_memory_space_constraint(slabs, pltpu.HBM)
    near, sent, diag = {}, {}, {}

    def direct(i):
        near[i] = [own[i], move(own[i], ahead), move(own[i], back)]

    def tie(*values):
        return list(lax.optimization_barrier(values))

    direct(0)
    for i in range(n):
        x0, p1, p2 = near[i]
        if i > 0:
            p1, p2, sent[i - 1] = tie(p1, p2, sent[i - 1])
        onward = move(p1, ahead)
        first = move(x0, swap)
        if i + 1 < n:
            p1, p2, onward, own[i + 1] = tie(p1, p2, onward, own[i + 1])
            direct(i + 1)
        else:
            p1, p2, onward = tie(p1, p2, onward)
        pieces = [x0, p1, p2, onward, first, move(p1, swap), move(p2, swap), move(onward, swap)]
        diag[i], sent[i] = product(pieces, held, place, sector, slot, dest_slot, cwt, nstr)
    out = None
    full = jax.ShapeDtypeStruct(ci.shape, ci.dtype)
    for i in range(n):
        recv = lax.all_to_all(sent[i], "str", split_axis=0, concat_axis=0, tiled=True)
        out = add(diag[i], recv, starts[i], full, out)
    return out


def solution(mesh):
    return jax.shard_map(
        body,
        mesh=mesh,
        in_specs=(
            P("str", None, None, "int"),
            P(None, None, None, "int"),
            P("str"),
            P("str", None),
            P("str"),
            P("str", None),
        ),
        out_specs=P("str", None, None, "int"),
        check_vma=False,
    )
```

profile of v0, /device:TPU:0, one launch (start us, length us, event | category | flops | bytes accessed | tf_op | source)
XLA Modules:
  0.0 138.9 jit_solution(15283782337712058003)
XLA Ops:
  0.0 1.4 %copy-done = bf16[12,128,2,256]{3,2,1,0:T(2,128)(2,1)S(1)} copy-done((bf16[12,128,2,256]{3,2,1,0:T(2,128)(2,1)S(1)}, bf16[12,128,2,256]{3,2,1,0:T(2,128)(2,1)}, u32[]{:S(2)}) %copy-start) | copy-done | bytes 1572888
  1.4 0.2 shard_map.64.refs_0_
  1.6 0.0 copy-start.12
  1.6 0.0 copy-start.13
  1.7 0.0 copy-start.10
  1.7 0.0 copy-start.11
  1.7 1.6 %collective-permute-start = (bf16[12,64,256]{2,1,0:T(8,128)(2,1)S(1)}, bf16[12,64,256]{2,1,0:T(8,128)(2,1)S(1)}, u32[]{:S(2)}, u32[]{:S(2)}) collective-permute-start(bf16[12,64,256]{2,1,0:T(8,128)(2,1)S(1)} %shard_map.64.refs_0_), channel_id=1, source_target_pairs={{0,2},{1,7},{2,4},{3,1},{4,6},{5,3},{6,0},{7,5},{8,10},{9,15},{10,... | collective-permute-start | bytes 1179656 | tf_op jit(solution)/shard_map/ppermute | solution.py:205
  3.3 1.7 %collective-permute-start.1 = (bf16[12,64,256]{2,1,0:T(8,128)(2,1)S(1)}, bf16[12,64,256]{2,1,0:T(8,128)(2,1)S(1)}, u32[]{:S(2)}, u32[]{:S(2)}) collective-permute-start(bf16[12,64,256]{2,1,0:T(8,128)(2,1)S(1)} %shard_map.64.refs_0_), channel_id=1, source_target_pairs={{0,6},{1,3},{2,0},{3,5},{4,2},{5,7},{6,4},{7,1},{8,14},{9,11},{10,... | collective-permute-start | bytes 1179656 | tf_op jit(solution)/shard_map/ppermute | solution.py:205
  5.0 8.5 %collective-permute-done.refs_1_ = bf16[12,64,256]{2,1,0:T(8,128)(2,1)S(1)} collective-permute-done((bf16[12,64,256]{2,1,0:T(8,128)(2,1)S(1)}, bf16[12,64,256]{2,1,0:T(8,128)(2,1)S(1)}, u32[]{:S(2)}, u32[]{:S(2)}) %collective-permute-start) | collective-permute-done | bytes 393248 | tf_op jit(solution)/shard_map/ppermute | solution.py:205
  13.5 1.7 %collective-permute-start.2 = (bf16[12,64,256]{2,1,0:T(8,128)(2,1)S(1)}, bf16[12,64,256]{2,1,0:T(8,128)(2,1)S(1)}, u32[]{:S(2)}, u32[]{:S(2)}) collective-permute-start(bf16[12,64,256]{2,1,0:T(8,128)(2,1)S(1)} %collective-permute-done.refs_1_), channel_id=1, source_target_pairs={{0,2},{1,7},{2,4},{3,1},{4,6},{5,3},{6,0},{7,5},{8,10},{9,15},{10,... | collective-permute-start | bytes 1179656 | tf_op jit(solution)/shard_map/ppermute | solution.py:205
  15.2 0.3 shard_map.65.refs_0_
  15.5 0.0 collective-permute-done.1.refs_2_
  15.5 6.9 %collective-permute-done.2.refs_3_ = bf16[12,64,256]{2,1,0:T(8,128)(2,1)S(1)} collective-permute-done((bf16[12,64,256]{2,1,0:T(8,128)(2,1)S(1)}, bf16[12,64,256]{2,1,0:T(8,128)(2,1)S(1)}, u32[]{:S(2)}, u32[]{:S(2)}) %collective-permute-start.2) | collective-permute-done | bytes 393248 | tf_op jit(solution)/shard_map/ppermute | solution.py:205
  22.5 0.0 collective-permute-start.6
  22.5 0.5 collective-permute-start.7
  23.0 0.0 collective-permute-start.8
  23.0 0.1 copy.10
  23.1 0.1 stack.35.place
  23.2 1.3 collective-permute-start.4
  24.5 0.0 collective-permute-done.5.refs_4_
  24.5 0.7 collective-permute-start.3
  25.2 0.2 convert_reduce_fusion
  25.4 0.0 collective-permute-done.8.refs_7_
  25.4 8.5 %shard_map.66 = (f32[12,64,256]{2,1,0:T(8,128)}, s16[16,144,256]{2,1,0:T(8,128)(2,1)}) custom-call(s32[8]{0:T(128)S(1)} %stack.35.place, s32[12]{0:T(128)S(1)} %copy-done.10, s32[12]{0:T(128)S(1)} %multiply_add_fusion.slot, s32[12]{0:T(128)S(1)} %copy-done.11, f32[12,2]{1,0:T(8,128)S(1)} %convert_element_type.7.coef, ...), custom_call_target="tpu_custom_call" | custom-call | flops 3221225472 | bytes 14680064 | tf_op jit(solution)/shard_map/pallas_call | solution.py:115
  33.9 0.0 copy-start.1
  34.0 5.2 %collective-permute-done.4.refs_2_ = bf16[12,96,256]{2,1,0:T(8,128)(2,1)S(1)} collective-permute-done((bf16[12,96,256]{2,1,0:T(8,128)(2,1)S(1)}, bf16[12,96,256]{2,1,0:T(8,128)(2,1)S(1)}, u32[]{:S(2)}, u32[]{:S(2)}) %collective-permute-start.4) | collective-permute-done | bytes 589856 | tf_op jit(solution)/shard_map/ppermute | solution.py:205
  39.1 1.1 collective-permute-done.3.refs_1_
  40.2 0.0 collective-permute-start.9
  40.2 1.3 collective-permute-start.12
  41.6 8.0 %all-to-all-start.2 = ((s16[16,144,256]{2,1,0:T(8,128)(2,1)}), s16[16,144,256]{2,1,0:T(8,128)(2,1)S(1)}, u32[]{:S(2)}, u32[]{:S(2)}) async-start(s16[16,144,256]{2,1,0:T(8,128)(2,1)} %get-tuple-element.50), calls=%async_computation.2 | async-start | bytes 2359296 | tf_op jit(solution)/shard_map/all_to_all | solution.py:236
  49.6 0.3 shard_map.67.refs_0_
  50.0 1.6 %collective-permute-done.9.refs_3_ = bf16[12,96,256]{2,1,0:T(8,128)(2,1)} collective-permute-done((bf16[12,96,256]{2,1,0:T(8,128)(2,1)}, bf16[12,96,256]{2,1,0:T(8,128)(2,1)}, u32[]{:S(2)}, u32[]{:S(2)}) %collective-permute-start.9) | collective-permute-done | bytes 589856 | tf_op jit(solution)/shard_map/ppermute | solution.py:205
  51.6 0.0 collective-permute-start.13
  51.7 0.5 collective-permute-start.14
  52.2 0.0 collective-permute-start.15
  52.2 1.1 collective-permute-start.11
  53.3 0.0 collective-permute-done.12.refs_4_
  53.3 0.9 collective-permute-start.10
  54.2 0.4 collective-permute-done.13.refs_5_
  54.6 0.3 collective-permute-done.14.refs_6_
  55.0 0.6 collective-permute-done.15.refs_7_
  55.5 10.5 %shard_map.68 = (f32[12,96,256]{2,1,0:T(8,128)}, s16[16,208,256]{2,1,0:T(8,128)(2,1)}) custom-call(s32[8]{0:T(128)S(1)} %stack.35.place, s32[12]{0:T(128)S(1)} %copy-done.10, s32[12]{0:T(128)S(1)} %multiply_add_fusion.slot, s32[12]{0:T(128)S(1)} %copy-done.11, f32[12,2]{1,0:T(8,128)S(1)} %convert_element_type.7.coef, ...), custom_call_target="tpu_custom_call" | custom-call | flops 4831838208 | bytes 14680064 | tf_op jit(solution)/shard_map/pallas_call | solution.py:115
  66.1 1.8 %collective-permute-done.11.refs_2_ = bf16[12,96,256]{2,1,0:T(8,128)(2,1)S(1)} collective-permute-done((bf16[12,96,256]{2,1,0:T(8,128)(2,1)S(1)}, bf16[12,96,256]{2,1,0:T(8,128)(2,1)S(1)}, u32[]{:S(2)}, u32[]{:S(2)}) %collective-permute-start.11) | collective-permute-done | bytes 589856 | tf_op jit(solution)/shard_map/ppermute | solution.py:205
  67.9 1.3 collective-permute-done.10.refs_1_
  69.2 0.0 collective-permute-start.16
  69.2 0.0 copy-start.2
  69.3 1.0 copy-done.2
  70.3 8.4 %all-to-all-start.1 = ((s16[16,208,256]{2,1,0:T(8,128)(2,1)}), s16[16,208,256]{2,1,0:T(8,128)(2,1)S(1)}, u32[]{:S(2)}, u32[]{:S(2)}) async-start(s16[16,208,256]{2,1,0:T(8,128)(2,1)} %get-tuple-element.48), calls=%async_computation.1 | async-start | bytes 3407872 | tf_op jit(solution)/shard_map/all_to_all | solution.py:236
  78.6 0.1 collective-permute-start.17
  78.7 1.9 %collective-permute-done.16.refs_3_ = bf16[12,96,256]{2,1,0:T(8,128)(2,1)} collective-permute-done((bf16[12,96,256]{2,1,0:T(8,128)(2,1)}, bf16[12,96,256]{2,1,0:T(8,128)(2,1)}, u32[]{:S(2)}, u32[]{:S(2)}) %collective-permute-start.16) | collective-permute-done | bytes 589856 | tf_op jit(solution)/shard_map/ppermute | solution.py:205
  80.6 0.5 collective-permute-start.19
  81.1 0.0 collective-permute-start.20
  81.2 2.5 %collective-permute-done.18.refs_5_ = bf16[12,96,256]{2,1,0:T(8,128)(2,1)S(1)} collective-permute-done((bf16[12,96,256]{2,1,0:T(8,128)(2,1)}, bf16[12,96,256]{2,1,0:T(8,128)(2,1)S(1)}, u32[]{:S(2)}, u32[]{:S(2)}) %collective-permute-start.18) | collective-permute-done | bytes 589856 | tf_op jit(solution)/shard_map/ppermute | solution.py:205
  83.6 0.3 collective-permute-done.19.refs_6_
  84.0 0.6 collective-permute-done.20.refs_7_
  84.5 10.3 %shard_map.69 = (f32[12,96,256]{2,1,0:T(8,128)}, s16[16,208,256]{2,1,0:T(8,128)(2,1)}) custom-call(s32[8]{0:T(128)S(1)} %stack.35.place, s32[12]{0:T(128)S(1)} %copy-done.10, s32[12]{0:T(128)S(1)} %multiply_add_fusion.slot, s32[12]{0:T(128)S(1)} %copy-done.11, f32[12,2]{1,0:T(8,128)S(1)} %convert_element_type.7.coef, bf16[12,96,256]{2,1,0:T(8,128)(2,1)S(1)} %copy-done.5, ...), custom_call_target="tpu_custom_call" | custom-call | flops 4831838208 | bytes 14680064 | tf_op jit(solution)/shard_map/pallas_call | solution.py:115
  94.8 11.1 %all-to-all-done.1.recv = s16[16,208,256]{2,1,0:T(8,128)(2,1)S(1)} async-done(((s16[16,208,256]{2,1,0:T(8,128)(2,1)}), s16[16,208,256]{2,1,0:T(8,128)(2,1)S(1)}, u32[]{:S(2)}, u32[]{:S(2)}) %all-to-all-start.1) | async-done | bytes 1703968 | tf_op jit(solution)/shard_map/all_to_all | solution.py:236
  106.0 3.7 %all-to-all-start = ((s16[16,208,256]{2,1,0:T(8,128)(2,1)}), s16[16,208,256]{2,1,0:T(8,128)(2,1)S(1)}, u32[]{:S(2)}, u32[]{:S(2)}) async-start(s16[16,208,256]{2,1,0:T(8,128)(2,1)} %get-tuple-element.46), calls=%async_computation | async-start | bytes 3407872 | tf_op jit(solution)/shard_map/all_to_all | solution.py:236
  109.7 0.0 copy-start.3
  109.7 1.3 copy-done.3
  111.0 3.4 %shard_map.70.refs_0_ = bf16[12,128,2,256]{3,2,1,0:T(2,128)(2,1)} custom-call(f32[12,64,256]{2,1,0:T(8,128)} %get-tuple-element.49.diag, s16[16,144,256]{2,1,0:T(8,128)(2,1)S(1)} %copy-done.3), custom_call_target="tpu_custom_call" | custom-call | tf_op jit(solution)/shard_map/pallas_call | solution.py:155
  114.4 3.7 %shard_map.71.refs_0_ = bf16[12,128,2,256]{3,2,1,0:T(2,128)(2,1)} custom-call(f32[12,96,256]{2,1,0:T(8,128)} %get-tuple-element.47.diag, s16[16,208,256]{2,1,0:T(8,128)(2,1)S(1)} %all-to-all-done.1.recv, bf16[12,128,2,256]{3,2,1,0:T(2,128)(2,1)} %shard_map.70.refs_0_), custom_call_target="tpu_custom_call", output_to_operand_aliasing={{}: (2, {})} | custom-call | tf_op jit(solution)/shard_map/pallas_call | solution.py:155
  118.1 17.0 %all-to-all-done.recv = s16[16,208,256]{2,1,0:T(8,128)(2,1)S(1)} async-done(((s16[16,208,256]{2,1,0:T(8,128)(2,1)}), s16[16,208,256]{2,1,0:T(8,128)(2,1)S(1)}, u32[]{:S(2)}, u32[]{:S(2)}) %all-to-all-start) | async-done | bytes 1703968 | tf_op jit(solution)/shard_map/all_to_all | solution.py:236
  135.2 3.7 %shard_map.72 = bf16[12,128,2,256]{3,2,1,0:T(2,128)(2,1)} custom-call(f32[12,96,256]{2,1,0:T(8,128)} %get-tuple-element.45.diag, s16[16,208,256]{2,1,0:T(8,128)(2,1)S(1)} %all-to-all-done.recv, bf16[12,128,2,256]{3,2,1,0:T(2,128)(2,1)} %shard_map.71.refs_0_), custom_call_target="tpu_custom_call", output_to_operand_aliasing={{}: (2, {})} | custom-call | tf_op jit(solution)/shard_map/pallas_call | solution.py:155
  (26 shorter events, 0.1 us)
Async XLA Ops:
  0.0 1.4 %copy-start = (bf16[12,128,2,256]{3,2,1,0:T(2,128)(2,1)S(1)}, bf16[12,128,2,256]{3,2,1,0:T(2,128)(2,1)}, u32[]{:S(2)}) copy-start(bf16[12,128,2,256]{3,2,1,0:T(2,128)(2,1)} %ci.5) | copy-start | bytes 4718596
  1.6 21.3 %copy-start.12 = (bf16[12,2]{0,1:T(2,128)(2,1)S(1)}, bf16[12,2]{0,1:T(2,128)(2,1)}, u32[]{:S(2)}) copy-start(bf16[12,2]{0,1:T(2,128)(2,1)} %param.11) | copy-start | bytes 148
  1.6 23.6 %copy-start.13 = (s32[12,1]{0,1:T(1,128)S(1)}, s32[12,1]{0,1:T(1,128)}, u32[]{:S(2)}) copy-start(s32[12,1]{0,1:T(1,128)} %param.9) | copy-start | bytes 148
  1.7 23.8 %copy-start.10 = (s32[12]{0:T(128)S(1)}, s32[12]{0:T(128)}, u32[]{:S(2)}) copy-start(s32[12]{0:T(128)} %sector.5) | copy-start | bytes 148
  1.7 23.8 %copy-start.11 = (s32[12]{0:T(128)S(1)}, s32[12]{0:T(128)}, u32[]{:S(2)}) copy-start(s32[12]{0:T(128)} %inner.5) | copy-start | bytes 148
  1.7 11.8 %collective-permute-start = (bf16[12,64,256]{2,1,0:T(8,128)(2,1)S(1)}, bf16[12,64,256]{2,1,0:T(8,128)(2,1)S(1)}, u32[]{:S(2)}, u32[]{:S(2)}) collective-permute-start(bf16[12,64,256]{2,1,0:T(8,128)(2,1)S(1)} %shard_map.64.refs_0_), channel_id=1, source_target_pairs={{0,2},{1,7},{2,4},{3,1},{4,6},{5,3},{6,0},{7,5},{8,10},{9,15},{10,... | collective-permute-start | bytes 1179656 | tf_op jit(solution)/shard_map/ppermute | solution.py:205
  3.3 12.2 %collective-permute-start.1 = (bf16[12,64,256]{2,1,0:T(8,128)(2,1)S(1)}, bf16[12,64,256]{2,1,0:T(8,128)(2,1)S(1)}, u32[]{:S(2)}, u32[]{:S(2)}) collective-permute-start(bf16[12,64,256]{2,1,0:T(8,128)(2,1)S(1)} %shard_map.64.refs_0_), channel_id=1, source_target_pairs={{0,6},{1,3},{2,0},{3,5},{4,2},{5,7},{6,4},{7,1},{8,14},{9,11},{10,... | collective-permute-start | bytes 1179656 | tf_op jit(solution)/shard_map/ppermute | solution.py:205
  13.5 9.0 %collective-permute-start.2 = (bf16[12,64,256]{2,1,0:T(8,128)(2,1)S(1)}, bf16[12,64,256]{2,1,0:T(8,128)(2,1)S(1)}, u32[]{:S(2)}, u32[]{:S(2)}) collective-permute-start(bf16[12,64,256]{2,1,0:T(8,128)(2,1)S(1)} %collective-permute-done.refs_1_), channel_id=1, source_target_pairs={{0,2},{1,7},{2,4},{3,1},{4,6},{5,3},{6,0},{7,5},{8,10},{9,15},{10,... | collective-permute-start | bytes 1179656 | tf_op jit(solution)/shard_map/ppermute | solution.py:205
  15.2 9.3 %collective-permute-start.5 = (bf16[12,64,256]{2,1,0:T(8,128)(2,1)S(1)}, bf16[12,64,256]{2,1,0:T(8,128)(2,1)S(1)}, u32[]{:S(2)}, u32[]{:S(2)}) collective-permute-start(bf16[12,64,256]{2,1,0:T(8,128)(2,1)S(1)} %shard_map.64.refs_0_), channel_id=1, source_target_pairs={{0,1},{1,0},{2,3},{3,2},{4,5},{5,4},{6,7},{7,6},{8,9},{9,8},{10,11... | collective-permute-start | bytes 1179656 | tf_op jit(solution)/shard_map/ppermute | solution.py:205
  22.5 2.9 %collective-permute-start.6 = (bf16[12,64,256]{2,1,0:T(8,128)(2,1)S(1)}, bf16[12,64,256]{2,1,0:T(8,128)(2,1)}, u32[]{:S(2)}, u32[]{:S(2)}) collective-permute-start(bf16[12,64,256]{2,1,0:T(8,128)(2,1)S(1)} %collective-permute-done.refs_1_), channel_id=1, source_target_pairs={{0,1},{1,0},{2,3},{3,2},{4,5},{5,4},{6,7},{7,6},{8,9},{9,8},{10,11... | collective-permute-start | bytes 1179656 | tf_op jit(solution)/shard_map/ppermute | solution.py:205
  22.5 3.0 %collective-permute-start.7 = (bf16[12,64,256]{2,1,0:T(8,128)(2,1)S(1)}, bf16[12,64,256]{2,1,0:T(8,128)(2,1)}, u32[]{:S(2)}, u32[]{:S(2)}) collective-permute-start(bf16[12,64,256]{2,1,0:T(8,128)(2,1)S(1)} %collective-permute-done.1.refs_2_), channel_id=1, source_target_pairs={{0,1},{1,0},{2,3},{3,2},{4,5},{5,4},{6,7},{7,6},{8,9},{9,8},{10,11... | collective-permute-start | bytes 1179656 | tf_op jit(solution)/shard_map/ppermute | solution.py:205
  23.0 2.5 %collective-permute-start.8 = (bf16[12,64,256]{2,1,0:T(8,128)(2,1)S(1)}, bf16[12,64,256]{2,1,0:T(8,128)(2,1)}, u32[]{:S(2)}, u32[]{:S(2)}) collective-permute-start(bf16[12,64,256]{2,1,0:T(8,128)(2,1)S(1)} %collective-permute-done.2.refs_3_), channel_id=1, source_target_pairs={{0,1},{1,0},{2,3},{3,2},{4,5},{5,4},{6,7},{7,6},{8,9},{9,8},{10,11... | collective-permute-start | bytes 1179656 | tf_op jit(solution)/shard_map/ppermute | solution.py:205
  23.2 16.0 %collective-permute-start.4 = (bf16[12,96,256]{2,1,0:T(8,128)(2,1)S(1)}, bf16[12,96,256]{2,1,0:T(8,128)(2,1)S(1)}, u32[]{:S(2)}, u32[]{:S(2)}) collective-permute-start(bf16[12,96,256]{2,1,0:T(8,128)(2,1)S(1)} %shard_map.65.refs_0_), channel_id=1, source_target_pairs={{0,6},{1,3},{2,0},{3,5},{4,2},{5,7},{6,4},{7,1},{8,14},{9,11},{10,... | collective-permute-start | bytes 1769480 | tf_op jit(solution)/shard_map/ppermute | solution.py:205
  24.5 15.7 %collective-permute-start.3 = (bf16[12,96,256]{2,1,0:T(8,128)(2,1)S(1)}, bf16[12,96,256]{2,1,0:T(8,128)(2,1)}, u32[]{:S(2)}, u32[]{:S(2)}) collective-permute-start(bf16[12,96,256]{2,1,0:T(8,128)(2,1)S(1)} %shard_map.65.refs_0_), channel_id=1, source_target_pairs={{0,2},{1,7},{2,4},{3,1},{4,6},{5,3},{6,0},{7,5},{8,10},{9,15},{10,... | collective-permute-start | bytes 1769480 | tf_op jit(solution)/shard_map/ppermute | solution.py:205
  33.9 15.7 %copy-start.1 = (bf16[12,128,2,256]{3,2,1,0:T(2,128)(2,1)S(1)}, bf16[12,128,2,256]{3,2,1,0:T(2,128)(2,1)}, u32[]{:S(2)}) copy-start(bf16[12,128,2,256]{3,2,1,0:T(2,128)(2,1)} %ci.5) | copy-start | bytes 4718596
  39.1 2.4 %copy-start.6 = (bf16[12,96,256]{2,1,0:T(8,128)(2,1)}, bf16[12,96,256]{2,1,0:T(8,128)(2,1)S(1)}, u32[]{:S(2)}) copy-start(bf16[12,96,256]{2,1,0:T(8,128)(2,1)S(1)} %collective-permute-done.4.refs_2_) | copy-start | bytes 1769476
  40.2 11.4 %collective-permute-start.9 = (bf16[12,96,256]{2,1,0:T(8,128)(2,1)}, bf16[12,96,256]{2,1,0:T(8,128)(2,1)}, u32[]{:S(2)}, u32[]{:S(2)}) collective-permute-start(bf16[12,96,256]{2,1,0:T(8,128)(2,1)} %collective-permute-done.3.refs_1_), channel_id=1, source_target_pairs={{0,2},{1,7},{2,4},{3,1},{4,6},{5,3},{6,0},{7,5},{8,10},{9,15},{10,... | collective-permute-start | bytes 1769480 | tf_op jit(solution)/shard_map/ppermute | solution.py:205
  40.2 13.1 %collective-permute-start.12 = (bf16[12,96,256]{2,1,0:T(8,128)(2,1)S(1)}, bf16[12,96,256]{2,1,0:T(8,128)(2,1)}, u32[]{:S(2)}, u32[]{:S(2)}) collective-permute-start(bf16[12,96,256]{2,1,0:T(8,128)(2,1)S(1)} %shard_map.65.refs_0_), channel_id=1, source_target_pairs={{0,1},{1,0},{2,3},{3,2},{4,5},{5,4},{6,7},{7,6},{8,9},{9,8},{10,11... | collective-permute-start | bytes 1769480 | tf_op jit(solution)/shard_map/ppermute | solution.py:205
  41.6 27.7 %all-to-all-start.2 = ((s16[16,144,256]{2,1,0:T(8,128)(2,1)}), s16[16,144,256]{2,1,0:T(8,128)(2,1)S(1)}, u32[]{:S(2)}, u32[]{:S(2)}) async-start(s16[16,144,256]{2,1,0:T(8,128)(2,1)} %get-tuple-element.50), calls=%async_computation.2 | async-start | bytes 2359296 | tf_op jit(solution)/shard_map/all_to_all | solution.py:236
  49.6 2.0 %copy-start.7 = (bf16[12,96,256]{2,1,0:T(8,128)(2,1)S(1)}, bf16[12,96,256]{2,1,0:T(8,128)(2,1)}, u32[]{:S(2)}) copy-start(bf16[12,96,256]{2,1,0:T(8,128)(2,1)} %copy-done.6) | copy-start | bytes 1769476
  50.0 16.1 %copy-start.4 = (bf16[12,96,256]{2,1,0:T(8,128)(2,1)}, bf16[12,96,256]{2,1,0:T(8,128)(2,1)S(1)}, u32[]{:S(2)}) copy-start(bf16[12,96,256]{2,1,0:T(8,128)(2,1)S(1)} %shard_map.67.refs_0_) | copy-start | bytes 1769476
  51.6 3.0 %collective-permute-start.13 = (bf16[12,96,256]{2,1,0:T(8,128)(2,1)}, bf16[12,96,256]{2,1,0:T(8,128)(2,1)S(1)}, u32[]{:S(2)}, u32[]{:S(2)}) collective-permute-start(bf16[12,96,256]{2,1,0:T(8,128)(2,1)} %collective-permute-done.3.refs_1_), channel_id=1, source_target_pairs={{0,1},{1,0},{2,3},{3,2},{4,5},{5,4},{6,7},{7,6},{8,9},{9,8},{10,11... | collective-permute-start | bytes 1769480 | tf_op jit(solution)/shard_map/ppermute | solution.py:205
  51.7 3.3 %collective-permute-start.14 = (bf16[12,96,256]{2,1,0:T(8,128)(2,1)S(1)}, bf16[12,96,256]{2,1,0:T(8,128)(2,1)S(1)}, u32[]{:S(2)}, u32[]{:S(2)}) collective-permute-start(bf16[12,96,256]{2,1,0:T(8,128)(2,1)S(1)} %copy-done.7), channel_id=1, source_target_pairs={{0,1},{1,0},{2,3},{3,2},{4,5},{5,4},{6,7},{7,6},{8,9},{9,8},{10,11... | collective-permute-start | bytes 1769480 | tf_op jit(solution)/shard_map/ppermute | solution.py:205
  52.2 3.4 %collective-permute-start.15 = (bf16[12,96,256]{2,1,0:T(8,128)(2,1)}, bf16[12,96,256]{2,1,0:T(8,128)(2,1)S(1)}, u32[]{:S(2)}, u32[]{:S(2)}) collective-permute-start(bf16[12,96,256]{2,1,0:T(8,128)(2,1)} %collective-permute-done.9.refs_3_), channel_id=1, source_target_pairs={{0,1},{1,0},{2,3},{3,2},{4,5},{5,4},{6,7},{7,6},{8,9},{9,8},{10,11... | collective-permute-start | bytes 1769480 | tf_op jit(solution)/shard_map/ppermute | solution.py:205
  52.2 15.7 %collective-permute-start.11 = (bf16[12,96,256]{2,1,0:T(8,128)(2,1)S(1)}, bf16[12,96,256]{2,1,0:T(8,128)(2,1)S(1)}, u32[]{:S(2)}, u32[]{:S(2)}) collective-permute-start(bf16[12,96,256]{2,1,0:T(8,128)(2,1)S(1)} %shard_map.67.refs_0_), channel_id=1, source_target_pairs={{0,6},{1,3},{2,0},{3,5},{4,2},{5,7},{6,4},{7,1},{8,14},{9,11},{10,... | collective-permute-start | bytes 1769480 | tf_op jit(solution)/shard_map/ppermute | solution.py:205
  53.3 15.9 %collective-permute-start.10 = (bf16[12,96,256]{2,1,0:T(8,128)(2,1)S(1)}, bf16[12,96,256]{2,1,0:T(8,128)(2,1)}, u32[]{:S(2)}, u32[]{:S(2)}) collective-permute-start(bf16[12,96,256]{2,1,0:T(8,128)(2,1)S(1)} %shard_map.67.refs_0_), channel_id=1, source_target_pairs={{0,2},{1,7},{2,4},{3,1},{4,6},{5,3},{6,0},{7,5},{8,10},{9,15},{10,... | collective-permute-start | bytes 1769480 | tf_op jit(solution)/shard_map/ppermute | solution.py:205
  67.9 1.3 copy-start.8
  69.2 9.4 %copy-start.5 = (bf16[12,96,256]{2,1,0:T(8,128)(2,1)S(1)}, bf16[12,96,256]{2,1,0:T(8,128)(2,1)}, u32[]{:S(2)}) copy-start(bf16[12,96,256]{2,1,0:T(8,128)(2,1)} %copy-done.4) | copy-start | bytes 1769476
  69.2 11.4 %collective-permute-start.16 = (bf16[12,96,256]{2,1,0:T(8,128)(2,1)}, bf16[12,96,256]{2,1,0:T(8,128)(2,1)}, u32[]{:S(2)}, u32[]{:S(2)}) collective-permute-start(bf16[12,96,256]{2,1,0:T(8,128)(2,1)} %collective-permute-done.10.refs_1_), channel_id=1, source_target_pairs={{0,2},{1,7},{2,4},{3,1},{4,6},{5,3},{6,0},{7,5},{8,10},{9,15},{10,... | collective-permute-start | bytes 1769480 | tf_op jit(solution)/shard_map/ppermute | solution.py:205
  69.2 1.0 copy-start.2
  70.3 10.4 %copy-start.9 = (bf16[12,96,256]{2,1,0:T(8,128)(2,1)S(1)}, bf16[12,96,256]{2,1,0:T(8,128)(2,1)}, u32[]{:S(2)}) copy-start(bf16[12,96,256]{2,1,0:T(8,128)(2,1)} %copy-done.8) | copy-start | bytes 1769476
  70.3 35.7 %all-to-all-start.1 = ((s16[16,208,256]{2,1,0:T(8,128)(2,1)}), s16[16,208,256]{2,1,0:T(8,128)(2,1)S(1)}, u32[]{:S(2)}, u32[]{:S(2)}) async-start(s16[16,208,256]{2,1,0:T(8,128)(2,1)} %get-tuple-element.48), calls=%async_computation.1 | async-start | bytes 3407872 | tf_op jit(solution)/shard_map/all_to_all | solution.py:236
  78.6 2.5 %collective-permute-start.17 = (bf16[12,96,256]{2,1,0:T(8,128)(2,1)S(1)}, bf16[12,96,256]{2,1,0:T(8,128)(2,1)S(1)}, u32[]{:S(2)}, u32[]{:S(2)}) collective-permute-start(bf16[12,96,256]{2,1,0:T(8,128)(2,1)S(1)} %copy-done.5), channel_id=1, source_target_pairs={{0,1},{1,0},{2,3},{3,2},{4,5},{5,4},{6,7},{7,6},{8,9},{9,8},{10,11... | collective-permute-start | bytes 1769480 | tf_op jit(solution)/shard_map/ppermute | solution.py:205
  80.6 3.0 %collective-permute-start.18 = (bf16[12,96,256]{2,1,0:T(8,128)(2,1)}, bf16[12,96,256]{2,1,0:T(8,128)(2,1)S(1)}, u32[]{:S(2)}, u32[]{:S(2)}) collective-permute-start(bf16[12,96,256]{2,1,0:T(8,128)(2,1)} %collective-permute-done.10.refs_1_), channel_id=1, source_target_pairs={{0,1},{1,0},{2,3},{3,2},{4,5},{5,4},{6,7},{7,6},{8,9},{9,8},{10,11... | collective-permute-start | bytes 1769480 | tf_op jit(solution)/shard_map/ppermute | solution.py:205
  80.6 3.3 %collective-permute-start.19 = (bf16[12,96,256]{2,1,0:T(8,128)(2,1)S(1)}, bf16[12,96,256]{2,1,0:T(8,128)(2,1)S(1)}, u32[]{:S(2)}, u32[]{:S(2)}) collective-permute-start(bf16[12,96,256]{2,1,0:T(8,128)(2,1)S(1)} %copy-done.9), channel_id=1, source_target_pairs={{0,1},{1,0},{2,3},{3,2},{4,5},{5,4},{6,7},{7,6},{8,9},{9,8},{10,11... | collective-permute-start | bytes 1769480 | tf_op jit(solution)/shard_map/ppermute | solution.py:205
  81.1 3.4 %collective-permute-start.20 = (bf16[12,96,256]{2,1,0:T(8,128)(2,1)}, bf16[12,96,256]{2,1,0:T(8,128)(2,1)S(1)}, u32[]{:S(2)}, u32[]{:S(2)}) collective-permute-start(bf16[12,96,256]{2,1,0:T(8,128)(2,1)} %collective-permute-done.16.refs_3_), channel_id=1, source_target_pairs={{0,1},{1,0},{2,3},{3,2},{4,5},{5,4},{6,7},{7,6},{8,9},{9,8},{10,11... | collective-permute-start | bytes 1769480 | tf_op jit(solution)/shard_map/ppermute | solution.py:205
  106.0 29.2 %all-to-all-start = ((s16[16,208,256]{2,1,0:T(8,128)(2,1)}), s16[16,208,256]{2,1,0:T(8,128)(2,1)S(1)}, u32[]{:S(2)}, u32[]{:S(2)}) async-start(s16[16,208,256]{2,1,0:T(8,128)(2,1)} %get-tuple-element.46), calls=%async_computation | async-start | bytes 3407872 | tf_op jit(solution)/shard_map/all_to_all | solution.py:236
  109.7 1.3 copy-start.3
where the time goes:
time: 140 us; the launch traced here: 139 us
  waiting for transfers between devices  61.3 us (44%)
  Pallas kernels  41 us (29%)
  starting transfers between devices  32.2 us (23%)
  local copies, waits for them, and re-layouts  3.92 us (3%)
    ppermute x21, waiting for transfers between devices, move(): return lax.ppermute(v, 'int', perm)  33.1 us
    pallas_call x3, Pallas kernels, product(): pl.pallas_call(product_kernel, grid_spec=grid, out_shape=[pltpu.HBM((nblk...  29.3 us
    all_to_all x3, waiting for transfers between devices, body(): lax.all_to_all(sent[i], 'str', split_axis=0, concat_axis=0, tiled=True)  28.2 us
    all_to_all x3, starting transfers between devices, body(): lax.all_to_all(sent[i], 'str', split_axis=0, concat_axis=0, tiled=True)  20.1 us
    ppermute x21, starting transfers between devices, move(): return lax.ppermute(v, 'int', perm)  12 us
    pallas_call x3, Pallas kernels, add(): pl.pallas_call(functools.partial(add_kernel, r0), in_specs=[hbm, vmem] +...  10.9 us
    unnamed x29, local copies, waits for them, and re-layouts  3.83 us
  transfers between devices with their start and end apart: 24, of which 16 were waited for; matrix products, arithmetic and copies ran while one was open for 0% of the time, Pallas kernels for 27%

commit v1 on v0

v1 whole, which is shorter than its diff:
```python
import functools

import jax
import jax.numpy as jnp
from jax import lax
from jax.experimental import pallas as pl
from jax.experimental.pallas import tpu as pltpu
from jax.sharding import PartitionSpec as P

CAP = 2
GROUPS = ((32,), (40,), (56,))
META = 16
LIMIT = 36 * 2**20
STEPS = 32000.0
MAGIC = 12582912.0
TILE = 16


def turn(y):
    rows, cols = y.shape
    z = y.reshape(rows // 8, 8, cols)
    even = lax.broadcasted_iota(jnp.int32, z.shape, 1) % 2 == 0
    after = pltpu.roll(z, 7, 1)
    before = pltpu.roll(z, 1, 1)
    return jnp.where(even, -after, before).reshape(rows, cols)


def split_kernel(r0, ci, out, buf, sem):
    load = pltpu.make_async_copy(ci.at[:, pl.ds(r0, buf.shape[1])], buf, sem)
    load.start()
    load.wait()
    out[...] = buf[...].reshape(out.shape)


def split(ci, r0, rc):
    nblk, rows, two, cols = ci.shape
    return pl.pallas_call(
        functools.partial(split_kernel, r0),
        in_specs=[pl.BlockSpec(memory_space=pltpu.HBM)],
        out_specs=pl.BlockSpec(memory_space=pltpu.VMEM),
        out_shape=jax.ShapeDtypeStruct((nblk, two * rc, cols), ci.dtype),
        scratch_shapes=[pltpu.VMEM((nblk, rc, two, cols), ci.dtype), pltpu.SemaphoreType.DMA],
        compiler_params=pltpu.CompilerParams(vmem_limit_bytes=LIMIT),
    )(ci)


def product_kernel(base, place, sector, slot, inner, coef, *refs):
    pieces, slab = refs[:8], refs[8]
    diag, send, acc, diags, part, codes, meta, sem = refs[-8:]
    s, c = pl.program_id(0), pl.program_id(1)
    nblk, rows, cols = diag.shape
    total = None
    for j, piece in enumerate(pieces):
        left = piece[...].reshape(nblk * rows, cols)
        right = slab[0, 0, pl.ds(pl.multiple_of(place[j] * cols, cols), cols), :]
        dot = jnp.dot(left, right, preferred_element_type=jnp.float32)
        total = dot if total is None else total + dot
    acc[s, c] = total.reshape(nblk, rows, cols)

    @pl.when((s == 1) & (c == 1))
    def _():
        line = lax.broadcasted_iota(jnp.int32, (META, cols), 0)
        half = line // (META // CAP)
        first_part = (line % (META // CAP)) < META // (2 * CAP)
        meta[...] = jnp.zeros(meta.shape, jnp.int16)
        levels = []
        for b in range(nblk):
            mine = sector[b]
            cr = coef[b, 0]
            ci = coef[b, 1]
            top = None
            for r in range(0, rows, TILE):
                span = pl.ds(r, TILE)
                diags[b, span] = acc[mine, 0, b, span] + turn(acc[mine, 1, b, span])
                p = acc[1 - mine, 0, b, span]
                q = acc[1 - mine, 1, b, span]
                value = (cr * p - ci * q) + turn(cr * q + ci * p)
                part[b, span] = value
                size = jnp.max(jnp.abs(value).reshape(TILE // 8, 8, cols), axis=0)
                top = size if top is None else jnp.maximum(top, size)
            top = jnp.max(top, axis=0, keepdims=True)
            level = jnp.ceil(jnp.log2(jnp.maximum(top, 1.2e-38)) * 256.0) + 1.0
            level = jnp.clip(level, -28160.0, 32766.0)
            levels.append(level)
            scale = STEPS / jnp.exp2(level * (1.0 / 256.0))
            for r in range(0, rows, TILE):
                code = (part[b, pl.ds(r, TILE)] * scale + MAGIC) - MAGIC
                row = (b % CAP) * rows + r
                codes[b // CAP, pl.ds(row, TILE), :] = code.astype(jnp.int32).astype(jnp.int16)
        copies = [pltpu.make_async_copy(diags, diag, sem.at[0])]
        copies[0].start()
        for b in range(nblk):
            dev = slot[b] // CAP
            cap = slot[b] % CAP
            first = pl.multiple_of(base + cap * rows, 16)
            pltpu.make_async_copy(
                codes.at[b // CAP, pl.ds((b % CAP) * rows, rows)], send.at[dev, pl.ds(first, rows)], sem.at[1]
            ).start()
        for b in range(nblk):
            dev = slot[b] // CAP
            cap = slot[b] % CAP
            old = meta[dev].astype(jnp.int32)
            new = jnp.where(first_part, levels[b].astype(jnp.int32), inner[b] + 1)
            meta[dev] = jnp.where(half == cap, new, old).astype(jnp.int16)
        last = pltpu.make_async_copy(meta, send.at[:, pl.ds(base + CAP * rows, META)], sem.at[2])
        last.start()
        pltpu.make_async_copy(diags, diag, sem.at[0]).wait()
        pltpu.make_async_copy(codes, send.at[pl.ds(0, nblk // CAP), pl.ds(base, CAP * rows)], sem.at[1]).wait()
        last.wait()


def product(pieces, slabs, place, sector, slot, inner, coef, base, shape, begun):
    nblk, rows, cols = pieces[0].shape
    vmem = pl.BlockSpec(memory_space=pltpu.VMEM)
    hbm = pl.BlockSpec(memory_space=pltpu.HBM)
    nstr = shape[0]
    rest = [] if begun is None else [begun]
    grid = pltpu.PrefetchScalarGridSpec(
        num_scalar_prefetch=5,
        grid=(2, 2),
        in_specs=[vmem] * 8 + [pl.BlockSpec((1, 1, slabs.shape[2], cols), lambda s, c, *_: (s, c, 0, 0))]
        + [hbm] * len(rest),
        out_specs=[hbm, hbm],
        scratch_shapes=[
            pltpu.VMEM((2, 2, nblk, rows, cols), jnp.float32),
            pltpu.VMEM((nblk, rows, cols), jnp.float32),
            pltpu.VMEM((nblk, rows, cols), jnp.float32),
            pltpu.VMEM((nblk // CAP, CAP * rows, cols), jnp.int16),
            pltpu.VMEM((nstr, META, cols), jnp.int16),
            pltpu.SemaphoreType.DMA((3,)),
        ],
    )
    return pl.pallas_call(
        functools.partial(product_kernel, base),
        grid_spec=grid,
        out_shape=[pltpu.HBM((nblk, rows, cols), jnp.float32), pltpu.HBM(shape, jnp.int16)],
        input_output_aliases={14: 1} if rest else {},
        compiler_params=pltpu.CompilerParams(vmem_limit_bytes=LIMIT),
        cost_estimate=pl.CostEstimate(
            flops=10**9, bytes_accessed=10**4, transcendentals=0
        ),
    )(place, sector, slot, inner, coef, *pieces, slabs, *rest)


def add_kernel(places, n, far, *refs):
    diags, recv = refs[:n], refs[n]
    scratch = refs[len(refs) - 3 * n - (3 if far else 1) :]
    out = refs[len(refs) - len(scratch) - 1]
    accs, dones, bufs, sem = scratch[:n], scratch[n : 2 * n], scratch[2 * n : 3 * n], scratch[-1]
    if far:
        codes, arrive = scratch[3 * n : 3 * n + 2]
        fetch = pltpu.make_async_copy(recv, codes, arrive)
        fetch.start()
        recv = codes
    loads = []
    for i in range(n):
        loads.append(pltpu.make_async_copy(diags[i], bufs[i], sem.at[i]))
        loads[i].start()
    stores = []
    base = 0
    for i in range(n):
        acc, done = accs[i], dones[i]
        nblk, rows, cols = diags[i].shape
        acc[...] = jnp.zeros(acc.shape, jnp.float32)
        if far and i == 0:
            fetch.wait()
        found = []
        info = base + CAP * rows
        for dev in range(recv.shape[0]):
            meta = recv[dev, info : info + META, :].astype(jnp.int32)
            for cap in range(CAP):
                at = cap * (META // CAP)
                found.append((dev, cap, meta[at + META // (2 * CAP), 0] - 1))
        for dev, cap, b in found:

            @pl.when(b >= 0)
            def _():
                at = cap * (META // CAP)
                meta = recv[dev, info : info + META, :].astype(jnp.int32)
                unit = jnp.exp2(meta[at : at + 1].astype(jnp.float32) * (1.0 / 256.0)) * (1.0 / STEPS)
                for r in range(0, rows, TILE):
                    line = base + cap * rows + r
                    code = recv[dev, line : line + TILE, :].astype(jnp.int32)
                    acc[b, pl.ds(r, TILE)] += code.astype(jnp.float32) * unit

        base += CAP * rows + META
        loads[i].wait()
        for b in range(nblk):
            done[b] = (acc[b] + bufs[i][b]).astype(done.dtype).reshape(done.shape[1:])
        store = pltpu.make_async_copy(done, out.at[:, pl.ds(places[i], rows // 2)], sem.at[n + i])
        store.start()
        stores.append(store)
    for store in stores:
        store.wait()


def add(diags, recv, places, full, out, far):
    n = len(diags)
    rest = [] if out is None else [out]
    vmem = pl.BlockSpec(memory_space=pltpu.VMEM)
    hbm = pl.BlockSpec(memory_space=pltpu.HBM)
    sums = [pltpu.VMEM(diag.shape, jnp.float32) for diag in diags]
    rounded = [pltpu.VMEM((d.shape[0], d.shape[1] // 2, 2, d.shape[2]), jnp.bfloat16) for d in diags]
    diags = [pltpu.with_memory_space_constraint(diag, pltpu.HBM) for diag in diags]
    codes = []
    if far:
        recv = pltpu.with_memory_space_constraint(recv, pltpu.HBM)
        codes = [pltpu.VMEM(recv.shape, recv.dtype), pltpu.SemaphoreType.DMA]
    return pl.pallas_call(
        functools.partial(add_kernel, places, n, far),
        in_specs=[hbm] * n + [hbm if far else vmem] + [hbm] * len(rest),
        out_specs=hbm,
        scratch_shapes=sums + rounded + sums + codes + [pltpu.SemaphoreType.DMA((2 * n,))],
        out_shape=pltpu.HBM(full.shape, full.dtype),
        input_output_aliases={n + 1: 0} if rest else {},
        compiler_params=pltpu.CompilerParams(vmem_limit_bytes=LIMIT),
    )(*diags, recv, *rest)


def body(ci, slabs, sector, dest_dev, dest_slot, coef):
    nblk, rows, two, ncol = ci.shape
    nstr = lax.axis_size("str")
    nint = lax.axis_size("int")
    nx = nint // 2
    here = lax.axis_index("int")
    x = here // 2
    core = here % 2

    def ipos(a, c):
        return (a % nx) * 2 + c

    def way(c):
        return 1 - 2 * c

    pairs = [(a, c) for a in range(nx) for c in range(2)]
    ahead = [(ipos(a, c), ipos(a + way(c), c)) for a, c in pairs]
    back = [(ipos(a, c), ipos(a - way(c), c)) for a, c in pairs]
    swap = [(ipos(a, c), ipos(a, 1 - c)) for a, c in pairs]

    d = way(core)
    place = jnp.stack(
        [
            ipos(x, core), ipos(x - d, core), ipos(x + d, core), ipos(x + 2, core),
            ipos(x, 1 - core), ipos(x + d, 1 - core), ipos(x - d, 1 - core), ipos(x + 2, 1 - core),
        ]
    ).astype(jnp.int32)

    target = dest_dev[:, 0]
    order = jnp.arange(nblk, dtype=jnp.int32)
    same = (target[:, None] == target[None, :]) & (order[:, None] > order[None, :])
    slot = target * CAP + jnp.sum(same.astype(jnp.int32), axis=1)
    cwt = coef.astype(jnp.float32)

    def move(v, perm):
        return lax.ppermute(v, "int", perm)

    sizes = [rc for group in GROUPS for rc in group]
    starts = [sum(sizes[:i]) for i in range(len(sizes))]
    n = len(sizes)
    raw = pltpu.with_memory_space_constraint(ci, pltpu.HBM)
    own = [split(raw, starts[i], sizes[i]) for i in range(n)]
    held = pltpu.with_memory_space_constraint(slabs, pltpu.HBM)

    def tie(*values):
        return list(lax.optimization_barrier(values))

    near = [[own[0], move(own[0], ahead), move(own[0], back)]]
    sent, diags, previous = [], [], None
    i = 0
    for group in GROUPS:
        shape = (nstr, sum(CAP * 2 * rc + META for rc in group), ncol)
        send, base, here_diags = None, 0, []
        for rc in group:
            x0, p1, p2 = near[i]
            if i > 0:
                p1, x0, _ = tie(p1, x0, previous)
            if i + 1 < n:
                own[i + 1], p1 = tie(own[i + 1], p1)
            onward = move(p1, ahead)
            first = move(x0, swap)
            p1s, p2s = move(p1, swap), move(p2, swap)
            if i + 1 < n:
                nxt, _, _ = tie(own[i + 1], p1, p2)
                near.append([nxt, move(nxt, ahead), move(nxt, back)])
            pieces = [x0, p1, p2, onward, first, p1s, p2s, move(onward, swap)]
            d, send = product(pieces, held, place, sector, slot, dest_slot, cwt, base, shape, send)
            here_diags.append(d)
            previous = d
            base += CAP * 2 * rc + META
            i += 1
        sent.append(send)
        diags.append(here_diags)
    full = jax.ShapeDtypeStruct(ci.shape, ci.dtype)
    out, i = None, 0
    for k, group in enumerate(GROUPS):
        recv = lax.all_to_all(sent[k], "str", split_axis=0, concat_axis=0, tiled=True)
        out = add(diags[k], recv, starts[i : i + len(group)], full, out, k + 1 < len(GROUPS))
        i += len(group)
    return out


def solution(mesh):
    return jax.shard_map(
        body,
        mesh=mesh,
        in_specs=(
            P("str", None, None, "int"),
            P(None, None, None, "int"),
            P("str"),
            P("str", None),
            P("str"),
            P("str", None),
        ),
        out_specs=P("str", None, None, "int"),
        check_vma=False,
    )
```

time: 140 us -> 131 us (0.936)
  waiting for transfers between devices: 61.3 us -> 56.7 us
  starting transfers between devices: 32.2 us -> 30.2 us
    ppermute x21, waiting for transfers between devices: 33.1 us -> 20.5 us  [move(): return lax.ppermute(v, 'int', perm)]
    all_to_all x3, waiting for transfers between devices: 28.2 us -> 36.2 us  [body(): lax.all_to_all(sent[k], 'str', split_axis=0, concat_axis=0, tiled=True)]
    all_to_all x3, starting transfers between devices: 20.1 us -> 16.4 us  [body(): lax.all_to_all(sent[k], 'str', split_axis=0, concat_axis=0, tiled=True)]
    ppermute x21, starting transfers between devices: 12 us -> 13.8 us  [move(): return lax.ppermute(v, 'int', perm)]
    unnamed x29 -> x23, local copies, waits for them, and re-layouts: 3.83 us -> 3.17 us
  transfers between devices with their start and end apart: 24 -> 24, of which waited for: 16 -> 10; matrix products, arithmetic and copies ran while one was open for 0% -> 0% of each run, Pallas kernels for 27% -> 28%
where the time goes in v1:
time: 131 us; the launch traced here: 130 us
  waiting for transfers between devices  56.7 us (43%)
  Pallas kernels  39.7 us (30%)
  starting transfers between devices  30.2 us (23%)
  local copies, waits for them, and re-layouts  3.26 us (2%)
    all_to_all x3, waiting for transfers between devices, body(): lax.all_to_all(sent[k], 'str', split_axis=0, concat_axis=0, tiled=True)  36.2 us
    pallas_call x3, Pallas kernels, product(): pl.pallas_call(functools.partial(product_kernel, base), grid_spec=grid, o...  28.3 us
    ppermute x21, waiting for transfers between devices, move(): return lax.ppermute(v, 'int', perm)  20.5 us
    all_to_all x3, starting transfers between devices, body(): lax.all_to_all(sent[k], 'str', split_axis=0, concat_axis=0, tiled=True)  16.4 us
    ppermute x21, starting transfers between devices, move(): return lax.ppermute(v, 'int', perm)  13.8 us
    pallas_call x3, Pallas kernels, add(): pl.pallas_call(functools.partial(add_kernel, places, n, far), in_specs=[h...  7.75 us
    pallas_call x3, Pallas kernels, split(): pl.pallas_call(functools.partial(split_kernel, r0), in_specs=[pl.BlockSpe...  3.67 us
    unnamed x23, local copies, waits for them, and re-layouts  3.17 us
  transfers between devices with their start and end apart: 24, of which 10 were waited for; matrix products, arithmetic and copies ran while one was open for 0% of the time, Pallas kernels for 28%

profile of v1, /device:TPU:0, one launch (start us, length us, event | category | flops | bytes accessed | tf_op | source)
XLA Modules:
  0.0 130.5 jit_solution(17532693945419167935)
XLA Ops:
  0.0 1.1 shard_map.66.refs_0_
  1.2 1.6 %collective-permute-start = (bf16[12,64,256]{2,1,0:T(8,128)(2,1)S(1)}, bf16[12,64,256]{2,1,0:T(8,128)(2,1)S(1)}, u32[]{:S(2)}, u32[]{:S(2)}) collective-permute-start(bf16[12,64,256]{2,1,0:T(8,128)(2,1)S(1)} %shard_map.66.refs_0_), channel_id=1, source_target_pairs={{0,2},{1,7},{2,4},{3,1},{4,6},{5,3},{6,0},{7,5},{8,10},{9,15},{10,... | collective-permute-start | bytes 1179656 | tf_op jit(solution)/shard_map/ppermute | solution.py:255
  2.8 1.7 %collective-permute-start.1 = (bf16[12,64,256]{2,1,0:T(8,128)(2,1)S(1)}, bf16[12,64,256]{2,1,0:T(8,128)(2,1)S(1)}, u32[]{:S(2)}, u32[]{:S(2)}) collective-permute-start(bf16[12,64,256]{2,1,0:T(8,128)(2,1)S(1)} %shard_map.66.refs_0_), channel_id=1, source_target_pairs={{0,6},{1,3},{2,0},{3,5},{4,2},{5,7},{6,4},{7,1},{8,14},{9,11},{10,... | collective-permute-start | bytes 1179656 | tf_op jit(solution)/shard_map/ppermute | solution.py:255
  4.5 1.2 shard_map.65.refs_0_
  5.7 0.0 copy-start.9
  5.7 0.0 copy-start.2
  5.7 0.0 copy-start.3
  5.7 7.2 %collective-permute-done.refs_1_ = bf16[12,64,256]{2,1,0:T(8,128)(2,1)S(1)} collective-permute-done((bf16[12,64,256]{2,1,0:T(8,128)(2,1)S(1)}, bf16[12,64,256]{2,1,0:T(8,128)(2,1)S(1)}, u32[]{:S(2)}, u32[]{:S(2)}) %collective-permute-start) | collective-permute-done | bytes 393248 | tf_op jit(solution)/shard_map/ppermute | solution.py:255
  12.9 1.7 %collective-permute-start.3 = (bf16[12,64,256]{2,1,0:T(8,128)(2,1)S(1)}, bf16[12,64,256]{2,1,0:T(8,128)(2,1)}, u32[]{:S(2)}, u32[]{:S(2)}) collective-permute-start(bf16[12,64,256]{2,1,0:T(8,128)(2,1)S(1)} %collective-permute-done.refs_1_), channel_id=1, source_target_pairs={{0,2},{1,7},{2,4},{3,1},{4,6},{5,3},{6,0},{7,5},{8,10},{9,15},{10,... | collective-permute-start | bytes 1179656 | tf_op jit(solution)/shard_map/ppermute | solution.py:255
  14.7 0.0 collective-permute-start.4
  14.7 0.0 collective-permute-done.1.refs_2_
  14.7 0.7 collective-permute-start.2
  15.4 1.0 collective-permute-start.5
  16.4 0.0 collective-permute-start.6
  16.4 5.6 %collective-permute-done.3.refs_3_ = bf16[12,64,256]{2,1,0:T(8,128)(2,1)} collective-permute-done((bf16[12,64,256]{2,1,0:T(8,128)(2,1)S(1)}, bf16[12,64,256]{2,1,0:T(8,128)(2,1)}, u32[]{:S(2)}, u32[]{:S(2)}) %collective-permute-start.3) | collective-permute-done | bytes 393248 | tf_op jit(solution)/shard_map/ppermute | solution.py:255
  22.0 0.0 collective-permute-start.7
  22.0 0.2 convert_reduce_fusion
  22.2 0.0 collective-permute-done.4.refs_4_
  22.2 0.0 copy-start
  22.2 0.7 copy-done
  23.0 1.3 %collective-permute-start.8 = (bf16[12,80,256]{2,1,0:T(8,128)(2,1)S(1)}, bf16[12,80,256]{2,1,0:T(8,128)(2,1)S(1)}, u32[]{:S(2)}, u32[]{:S(2)}) collective-permute-start(bf16[12,80,256]{2,1,0:T(8,128)(2,1)S(1)} %shard_map.65.refs_0_), channel_id=1, source_target_pairs={{0,6},{1,3},{2,0},{3,5},{4,2},{5,7},{6,4},{7,1},{8,14},{9,11},{10,... | collective-permute-start | bytes 1474568 | tf_op jit(solution)/shard_map/ppermute | solution.py:255
  24.3 1.3 %shard_map.64.refs_0_ = bf16[12,112,256]{2,1,0:T(8,128)(2,1)S(1)} custom-call(bf16[12,128,2,256]{3,2,1,0:T(2,128)(2,1)} %ci.5), custom_call_target="tpu_custom_call" | custom-call | tf_op jit(solution)/shard_map/pallas_call | solution.py:37
  25.6 0.1 copy.10
  25.7 0.1 stack.35.place
  25.8 0.0 collective-permute-done.6.refs_6_
  25.9 0.0 collective-permute-done.5.refs_5_
  25.9 0.0 collective-permute-done.7.refs_7_
  25.9 0.0 copy-start.1
  25.9 1.0 copy-done.1
  26.9 8.6 %shard_map.67 = (f32[12,64,256]{2,1,0:T(8,128)}, s16[16,144,256]{2,1,0:T(8,128)(2,1)}) custom-call(s32[8]{0:T(128)S(1)} %stack.35.place, s32[12]{0:T(128)S(1)} %copy-done.2, s32[12]{0:T(128)S(1)} %multiply_add_fusion.slot, s32[12]{0:T(128)S(1)} %copy-done.3, f32[12,2]{1,0:T(8,128)S(1)} %convert_element_type.7.coef, ...), custom_call_target="tpu_custom_call" | custom-call | flops 1000000000 | bytes 10000 | tf_op jit(solution)/shard_map/pallas_call | solution.py:133
  35.5 0.0 collective-permute-done.2.refs_1_
  35.5 0.8 collective-permute-start.10
  36.2 8.3 %all-to-all-start.2 = ((s16[16,144,256]{2,1,0:T(8,128)(2,1)}), s16[16,144,256]{2,1,0:T(8,128)(2,1)}, u32[]{:S(2)}, u32[]{:S(2)}) async-start(s16[16,144,256]{2,1,0:T(8,128)(2,1)} %get-tuple-element.36), calls=%async_computation.2 | async-start | bytes 2359296 | tf_op jit(solution)/shard_map/all_to_all | solution.py:296
  44.5 0.0 collective-permute-done.8.refs_2_
  44.5 0.4 collective-permute-start.9
  44.9 0.6 collective-permute-start.13
  45.6 0.1 collective-permute-start.12
  45.7 0.4 collective-permute-start.11
  46.1 0.1 collective-permute-start.14
  46.2 0.9 collective-permute-done.13.refs_6_
  47.0 2.6 %collective-permute-start.15 = (bf16[12,112,256]{2,1,0:T(8,128)(2,1)S(1)}, bf16[12,112,256]{2,1,0:T(8,128)(2,1)S(1)}, u32[]{:S(2)}, u32[]{:S(2)}) collective-permute-start(bf16[12,112,256]{2,1,0:T(8,128)(2,1)S(1)} %shard_map.64.refs_0_), channel_id=1, source_target_pairs={{0,6},{1,3},{2,0},{3,5},{4,2},{5,7},{6,4},{7,1},{8,14},{9,11},{10,... | collective-permute-start | bytes 2064392 | tf_op jit(solution)/shard_map/ppermute | solution.py:255
  49.7 0.0 copy-start.4
  49.7 0.6 copy-done.4
  50.4 0.7 copy-done.7
  51.0 8.8 %shard_map.68 = (f32[12,80,256]{2,1,0:T(8,128)}, s16[16,176,256]{2,1,0:T(8,128)(2,1)}) custom-call(s32[8]{0:T(128)S(1)} %stack.35.place, s32[12]{0:T(128)S(1)} %copy-done.2, s32[12]{0:T(128)S(1)} %copy-done.7, s32[12]{0:T(128)S(1)} %copy-done.4, f32[12,2]{1,0:T(8,128)S(1)} %convert_element_type.7.coef, bf16[12,80,256]{2,1,0:T(8,128)(2,1)S(1)} %shard_map.65.refs_0_, ...), custom_call_target="tpu_custom_call" | custom-call | flops 1000000000 | bytes 10000 | tf_op jit(solution)/shard_map/pallas_call | solution.py:133
  59.9 0.0 copy-start.5
  59.9 2.3 %collective-permute-done.9.refs_1_ = bf16[12,112,256]{2,1,0:T(8,128)(2,1)S(1)} collective-permute-done((bf16[12,112,256]{2,1,0:T(8,128)(2,1)S(1)}, bf16[12,112,256]{2,1,0:T(8,128)(2,1)S(1)}, u32[]{:S(2)}, u32[]{:S(2)}) %collective-permute-start.9) | collective-permute-done | bytes 688160 | tf_op jit(solution)/shard_map/ppermute | solution.py:255
  62.2 5.0 %all-to-all-done.2.refs_1_ = s16[16,144,256]{2,1,0:T(8,128)(2,1)} async-done(((s16[16,144,256]{2,1,0:T(8,128)(2,1)}), s16[16,144,256]{2,1,0:T(8,128)(2,1)}, u32[]{:S(2)}, u32[]{:S(2)}) %all-to-all-start.2) | async-done | bytes 1179680 | tf_op jit(solution)/shard_map/all_to_all | solution.py:296
  67.2 4.4 %all-to-all-start.1 = ((s16[16,176,256]{2,1,0:T(8,128)(2,1)}), s16[16,176,256]{2,1,0:T(8,128)(2,1)}, u32[]{:S(2)}, u32[]{:S(2)}) async-start(s16[16,176,256]{2,1,0:T(8,128)(2,1)} %get-tuple-element.35), calls=%async_computation.1 | async-start | bytes 2883584 | tf_op jit(solution)/shard_map/all_to_all | solution.py:296
  71.6 0.0 collective-permute-done.15.refs_2_
  71.6 0.1 collective-permute-start.19
  71.7 0.5 collective-permute-start.18
  72.2 0.1 collective-permute-start.17
  72.3 2.0 %collective-permute-done.16.refs_3_ = bf16[12,112,256]{2,1,0:T(8,128)(2,1)S(1)} collective-permute-done((bf16[12,112,256]{2,1,0:T(8,128)(2,1)S(1)}, bf16[12,112,256]{2,1,0:T(8,128)(2,1)S(1)}, u32[]{:S(2)}, u32[]{:S(2)}) %collective-permute-start.16) | collective-permute-done | bytes 688160 | tf_op jit(solution)/shard_map/ppermute | solution.py:255
  74.3 0.0 collective-permute-start.20
  74.3 1.5 %collective-permute-done.17.refs_4_ = bf16[12,112,256]{2,1,0:T(8,128)(2,1)S(1)} collective-permute-done((bf16[12,112,256]{2,1,0:T(8,128)(2,1)S(1)}, bf16[12,112,256]{2,1,0:T(8,128)(2,1)S(1)}, u32[]{:S(2)}, u32[]{:S(2)}) %collective-permute-start.17) | collective-permute-done | bytes 688160 | tf_op jit(solution)/shard_map/ppermute | solution.py:255
  75.8 1.0 collective-permute-done.20.refs_7_
  76.8 10.9 %shard_map.69 = (f32[12,112,256]{2,1,0:T(8,128)}, s16[16,240,256]{2,1,0:T(8,128)(2,1)}) custom-call(s32[8]{0:T(128)S(1)} %stack.35.place, s32[12]{0:T(128)S(1)} %copy-done.2, s32[12]{0:T(128)S(1)} %copy-done.8, s32[12]{0:T(128)S(1)} %copy-done.5, f32[12,2]{1,0:T(8,128)S(1)} %convert_element_type.7.coef, bf16[12,112,256]{2,1,0:T(8,128)(2,1)S(1)} %shard_map.64.refs_0_, ...), custom_call_target="tpu_custom_call" | custom-call | flops 1000000000 | bytes 10000 | tf_op jit(solution)/shard_map/pallas_call | solution.py:133
  87.7 7.6 %all-to-all-done.1.refs_1_ = s16[16,176,256]{2,1,0:T(8,128)(2,1)} async-done(((s16[16,176,256]{2,1,0:T(8,128)(2,1)}), s16[16,176,256]{2,1,0:T(8,128)(2,1)}, u32[]{:S(2)}, u32[]{:S(2)}) %all-to-all-start.1) | async-done | bytes 1441824 | tf_op jit(solution)/shard_map/all_to_all | solution.py:296
  95.3 3.7 %all-to-all-start = ((s16[16,240,256]{2,1,0:T(8,128)(2,1)}), s16[16,240,256]{2,1,0:T(8,128)(2,1)S(1)}, u32[]{:S(2)}, u32[]{:S(2)}) async-start(s16[16,240,256]{2,1,0:T(8,128)(2,1)} %get-tuple-element.34), calls=%async_computation | async-start | bytes 3932160 | tf_op jit(solution)/shard_map/all_to_all | solution.py:296
  99.0 2.6 %shard_map.70.refs_2_ = bf16[12,128,2,256]{3,2,1,0:T(2,128)(2,1)} custom-call(f32[12,64,256]{2,1,0:T(8,128)} %get-tuple-element.24.refs_0_, s16[16,144,256]{2,1,0:T(8,128)(2,1)} %all-to-all-done.2.refs_1_), custom_call_target="tpu_custom_call" | custom-call | tf_op jit(solution)/shard_map/pallas_call | solution.py:209
  101.6 2.7 %shard_map.71.refs_2_ = bf16[12,128,2,256]{3,2,1,0:T(2,128)(2,1)} custom-call(f32[12,80,256]{2,1,0:T(8,128)} %get-tuple-element.30.refs_0_, s16[16,176,256]{2,1,0:T(8,128)(2,1)} %all-to-all-done.1.refs_1_, bf16[12,128,2,256]{3,2,1,0:T(2,128)(2,1)} %shard_map.70.refs_2_), custom_call_target="tpu_custom_call", output_to_operand_aliasing={{}: (2, {})} | custom-call | tf_op jit(solution)/shard_map/pallas_call | solution.py:209
  104.3 23.5 %all-to-all-done.refs_1_ = s16[16,240,256]{2,1,0:T(8,128)(2,1)S(1)} async-done(((s16[16,240,256]{2,1,0:T(8,128)(2,1)}), s16[16,240,256]{2,1,0:T(8,128)(2,1)S(1)}, u32[]{:S(2)}, u32[]{:S(2)}) %all-to-all-start) | async-done | bytes 1966112 | tf_op jit(solution)/shard_map/all_to_all | solution.py:296
  127.9 2.5 %shard_map.72 = bf16[12,128,2,256]{3,2,1,0:T(2,128)(2,1)} custom-call(f32[12,112,256]{2,1,0:T(8,128)} %get-tuple-element.33.refs_0_, s16[16,240,256]{2,1,0:T(8,128)(2,1)S(1)} %all-to-all-done.refs_1_, bf16[12,128,2,256]{3,2,1,0:T(2,128)(2,1)} %shard_map.71.refs_2_), custom_call_target="tpu_custom_call", output_to_operand_aliasing={{}: (2, {})} | custom-call | tf_op jit(solution)/shard_map/pallas_call | solution.py:209
  (20 shorter events, 0.0 us)
Async XLA Ops:
  0.0 22.0 %copy-start.10 = (s32[12,1]{0,1:T(1,128)S(1)}, s32[12,1]{0,1:T(1,128)}, u32[]{:S(2)}) copy-start(s32[12,1]{0,1:T(1,128)} %param.9) | copy-start | bytes 148
  1.2 11.8 %collective-permute-start = (bf16[12,64,256]{2,1,0:T(8,128)(2,1)S(1)}, bf16[12,64,256]{2,1,0:T(8,128)(2,1)S(1)}, u32[]{:S(2)}, u32[]{:S(2)}) collective-permute-start(bf16[12,64,256]{2,1,0:T(8,128)(2,1)S(1)} %shard_map.66.refs_0_), channel_id=1, source_target_pairs={{0,2},{1,7},{2,4},{3,1},{4,6},{5,3},{6,0},{7,5},{8,10},{9,15},{10,... | collective-permute-start | bytes 1179656 | tf_op jit(solution)/shard_map/ppermute | solution.py:255
  2.8 11.9 %collective-permute-start.1 = (bf16[12,64,256]{2,1,0:T(8,128)(2,1)S(1)}, bf16[12,64,256]{2,1,0:T(8,128)(2,1)S(1)}, u32[]{:S(2)}, u32[]{:S(2)}) collective-permute-start(bf16[12,64,256]{2,1,0:T(8,128)(2,1)S(1)} %shard_map.66.refs_0_), channel_id=1, source_target_pairs={{0,6},{1,3},{2,0},{3,5},{4,2},{5,7},{6,4},{7,1},{8,14},{9,11},{10,... | collective-permute-start | bytes 1179656 | tf_op jit(solution)/shard_map/ppermute | solution.py:255
  5.7 20.0 %copy-start.9 = (bf16[12,2]{0,1:T(2,128)(2,1)S(1)}, bf16[12,2]{0,1:T(2,128)(2,1)}, u32[]{:S(2)}) copy-start(bf16[12,2]{0,1:T(2,128)(2,1)} %param.11) | copy-start | bytes 148
  5.7 20.2 %copy-start.2 = (s32[12]{0:T(128)S(1)}, s32[12]{0:T(128)}, u32[]{:S(2)}) copy-start(s32[12]{0:T(128)} %sector.5) | copy-start | bytes 148
  5.7 20.2 %copy-start.3 = (s32[12]{0:T(128)S(1)}, s32[12]{0:T(128)}, u32[]{:S(2)}) copy-start(s32[12]{0:T(128)} %inner.5) | copy-start | bytes 148
  12.9 9.1 %collective-permute-start.3 = (bf16[12,64,256]{2,1,0:T(8,128)(2,1)S(1)}, bf16[12,64,256]{2,1,0:T(8,128)(2,1)}, u32[]{:S(2)}, u32[]{:S(2)}) collective-permute-start(bf16[12,64,256]{2,1,0:T(8,128)(2,1)S(1)} %collective-permute-done.refs_1_), channel_id=1, source_target_pairs={{0,2},{1,7},{2,4},{3,1},{4,6},{5,3},{6,0},{7,5},{8,10},{9,15},{10,... | collective-permute-start | bytes 1179656 | tf_op jit(solution)/shard_map/ppermute | solution.py:255
  14.7 7.6 %collective-permute-start.4 = (bf16[12,64,256]{2,1,0:T(8,128)(2,1)S(1)}, bf16[12,64,256]{2,1,0:T(8,128)(2,1)S(1)}, u32[]{:S(2)}, u32[]{:S(2)}) collective-permute-start(bf16[12,64,256]{2,1,0:T(8,128)(2,1)S(1)} %shard_map.66.refs_0_), channel_id=1, source_target_pairs={{0,1},{1,0},{2,3},{3,2},{4,5},{5,4},{6,7},{7,6},{8,9},{9,8},{10,11... | collective-permute-start | bytes 1179656 | tf_op jit(solution)/shard_map/ppermute | solution.py:255
  14.7 20.8 %collective-permute-start.2 = (bf16[12,80,256]{2,1,0:T(8,128)(2,1)S(1)}, bf16[12,80,256]{2,1,0:T(8,128)(2,1)S(1)}, u32[]{:S(2)}, u32[]{:S(2)}) collective-permute-start(bf16[12,80,256]{2,1,0:T(8,128)(2,1)S(1)} %shard_map.65.refs_0_), channel_id=1, source_target_pairs={{0,2},{1,7},{2,4},{3,1},{4,6},{5,3},{6,0},{7,5},{8,10},{9,15},{10,... | collective-permute-start | bytes 1474568 | tf_op jit(solution)/shard_map/ppermute | solution.py:255
  15.4 10.4 %collective-permute-start.5 = (bf16[12,64,256]{2,1,0:T(8,128)(2,1)S(1)}, bf16[12,64,256]{2,1,0:T(8,128)(2,1)}, u32[]{:S(2)}, u32[]{:S(2)}) collective-permute-start(bf16[12,64,256]{2,1,0:T(8,128)(2,1)S(1)} %collective-permute-done.refs_1_), channel_id=1, source_target_pairs={{0,1},{1,0},{2,3},{3,2},{4,5},{5,4},{6,7},{7,6},{8,9},{9,8},{10,11... | collective-permute-start | bytes 1179656 | tf_op jit(solution)/shard_map/ppermute | solution.py:255
  16.4 9.4 %collective-permute-start.6 = (bf16[12,64,256]{2,1,0:T(8,128)(2,1)S(1)}, bf16[12,64,256]{2,1,0:T(8,128)(2,1)}, u32[]{:S(2)}, u32[]{:S(2)}) collective-permute-start(bf16[12,64,256]{2,1,0:T(8,128)(2,1)S(1)} %collective-permute-done.1.refs_2_), channel_id=1, source_target_pairs={{0,1},{1,0},{2,3},{3,2},{4,5},{5,4},{6,7},{7,6},{8,9},{9,8},{10,11... | collective-permute-start | bytes 1179656 | tf_op jit(solution)/shard_map/ppermute | solution.py:255
  22.0 3.8 %collective-permute-start.7 = (bf16[12,64,256]{2,1,0:T(8,128)(2,1)}, bf16[12,64,256]{2,1,0:T(8,128)(2,1)}, u32[]{:S(2)}, u32[]{:S(2)}) collective-permute-start(bf16[12,64,256]{2,1,0:T(8,128)(2,1)} %collective-permute-done.3.refs_3_), channel_id=1, source_target_pairs={{0,1},{1,0},{2,3},{3,2},{4,5},{5,4},{6,7},{7,6},{8,9},{9,8},{10,11... | collective-permute-start | bytes 1179656 | tf_op jit(solution)/shard_map/ppermute | solution.py:255
  22.2 0.7 copy-start
  23.0 21.5 %collective-permute-start.8 = (bf16[12,80,256]{2,1,0:T(8,128)(2,1)S(1)}, bf16[12,80,256]{2,1,0:T(8,128)(2,1)S(1)}, u32[]{:S(2)}, u32[]{:S(2)}) collective-permute-start(bf16[12,80,256]{2,1,0:T(8,128)(2,1)S(1)} %shard_map.65.refs_0_), channel_id=1, source_target_pairs={{0,6},{1,3},{2,0},{3,5},{4,2},{5,7},{6,4},{7,1},{8,14},{9,11},{10,... | collective-permute-start | bytes 1474568 | tf_op jit(solution)/shard_map/ppermute | solution.py:255
  24.3 11.2 %copy-start.6 = (s32[12]{0:T(128)}, s32[12]{0:T(128)S(1)}, u32[]{:S(2)}) copy-start(s32[12]{0:T(128)S(1)} %multiply_add_fusion.slot) | copy-start | bytes 148
  25.9 1.0 copy-start.1
  35.5 10.6 %collective-permute-start.10 = (bf16[12,80,256]{2,1,0:T(8,128)(2,1)S(1)}, bf16[12,80,256]{2,1,0:T(8,128)(2,1)}, u32[]{:S(2)}, u32[]{:S(2)}) collective-permute-start(bf16[12,80,256]{2,1,0:T(8,128)(2,1)S(1)} %collective-permute-done.2.refs_1_), channel_id=1, source_target_pairs={{0,2},{1,7},{2,4},{3,1},{4,6},{5,3},{6,0},{7,5},{8,10},{9,15},{10,... | collective-permute-start | bytes 1474568 | tf_op jit(solution)/shard_map/ppermute | solution.py:255
  36.2 31.0 %all-to-all-start.2 = ((s16[16,144,256]{2,1,0:T(8,128)(2,1)}), s16[16,144,256]{2,1,0:T(8,128)(2,1)}, u32[]{:S(2)}, u32[]{:S(2)}) async-start(s16[16,144,256]{2,1,0:T(8,128)(2,1)} %get-tuple-element.36), calls=%async_computation.2 | async-start | bytes 2359296 | tf_op jit(solution)/shard_map/all_to_all | solution.py:296
  44.5 17.7 %collective-permute-start.9 = (bf16[12,112,256]{2,1,0:T(8,128)(2,1)S(1)}, bf16[12,112,256]{2,1,0:T(8,128)(2,1)S(1)}, u32[]{:S(2)}, u32[]{:S(2)}) collective-permute-start(bf16[12,112,256]{2,1,0:T(8,128)(2,1)S(1)} %shard_map.64.refs_0_), channel_id=1, source_target_pairs={{0,2},{1,7},{2,4},{3,1},{4,6},{5,3},{6,0},{7,5},{8,10},{9,15},{10,... | collective-permute-start | bytes 2064392 | tf_op jit(solution)/shard_map/ppermute | solution.py:255
  44.9 2.1 %collective-permute-start.13 = (bf16[12,80,256]{2,1,0:T(8,128)(2,1)S(1)}, bf16[12,80,256]{2,1,0:T(8,128)(2,1)S(1)}, u32[]{:S(2)}, u32[]{:S(2)}) collective-permute-start(bf16[12,80,256]{2,1,0:T(8,128)(2,1)S(1)} %collective-permute-done.8.refs_2_), channel_id=1, source_target_pairs={{0,1},{1,0},{2,3},{3,2},{4,5},{5,4},{6,7},{7,6},{8,9},{9,8},{10,11... | collective-permute-start | bytes 1474568 | tf_op jit(solution)/shard_map/ppermute | solution.py:255
  45.6 4.1 %collective-permute-start.12 = (bf16[12,80,256]{2,1,0:T(8,128)(2,1)S(1)}, bf16[12,80,256]{2,1,0:T(8,128)(2,1)S(1)}, u32[]{:S(2)}, u32[]{:S(2)}) collective-permute-start(bf16[12,80,256]{2,1,0:T(8,128)(2,1)S(1)} %collective-permute-done.2.refs_1_), channel_id=1, source_target_pairs={{0,1},{1,0},{2,3},{3,2},{4,5},{5,4},{6,7},{7,6},{8,9},{9,8},{10,11... | collective-permute-start | bytes 1474568 | tf_op jit(solution)/shard_map/ppermute | solution.py:255
  45.7 4.0 %collective-permute-start.11 = (bf16[12,80,256]{2,1,0:T(8,128)(2,1)S(1)}, bf16[12,80,256]{2,1,0:T(8,128)(2,1)S(1)}, u32[]{:S(2)}, u32[]{:S(2)}) collective-permute-start(bf16[12,80,256]{2,1,0:T(8,128)(2,1)S(1)} %shard_map.65.refs_0_), channel_id=1, source_target_pairs={{0,1},{1,0},{2,3},{3,2},{4,5},{5,4},{6,7},{7,6},{8,9},{9,8},{10,11... | collective-permute-start | bytes 1474568 | tf_op jit(solution)/shard_map/ppermute | solution.py:255
  46.1 3.6 %collective-permute-start.14 = (bf16[12,80,256]{2,1,0:T(8,128)(2,1)}, bf16[12,80,256]{2,1,0:T(8,128)(2,1)S(1)}, u32[]{:S(2)}, u32[]{:S(2)}) collective-permute-start(bf16[12,80,256]{2,1,0:T(8,128)(2,1)} %collective-permute-done.10.refs_3_), channel_id=1, source_target_pairs={{0,1},{1,0},{2,3},{3,2},{4,5},{5,4},{6,7},{7,6},{8,9},{9,8},{10,11... | collective-permute-start | bytes 1474568 | tf_op jit(solution)/shard_map/ppermute | solution.py:255
  47.0 24.6 %collective-permute-start.15 = (bf16[12,112,256]{2,1,0:T(8,128)(2,1)S(1)}, bf16[12,112,256]{2,1,0:T(8,128)(2,1)S(1)}, u32[]{:S(2)}, u32[]{:S(2)}) collective-permute-start(bf16[12,112,256]{2,1,0:T(8,128)(2,1)S(1)} %shard_map.64.refs_0_), channel_id=1, source_target_pairs={{0,6},{1,3},{2,0},{3,5},{4,2},{5,7},{6,4},{7,1},{8,14},{9,11},{10,... | collective-permute-start | bytes 2064392 | tf_op jit(solution)/shard_map/ppermute | solution.py:255
  49.7 0.7 copy-start.4
  50.4 0.7 copy-start.7
  59.9 16.9 %copy-start.5 = (s32[12]{0:T(128)S(1)}, s32[12]{0:T(128)}, u32[]{:S(2)}) copy-start(s32[12]{0:T(128)} %inner.5) | copy-start | bytes 148
  59.9 16.9 %copy-start.8 = (s32[12]{0:T(128)S(1)}, s32[12]{0:T(128)}, u32[]{:S(2)}) copy-start(s32[12]{0:T(128)} %copy-done.6) | copy-start | bytes 148
  62.2 12.1 %collective-permute-start.16 = (bf16[12,112,256]{2,1,0:T(8,128)(2,1)S(1)}, bf16[12,112,256]{2,1,0:T(8,128)(2,1)S(1)}, u32[]{:S(2)}, u32[]{:S(2)}) collective-permute-start(bf16[12,112,256]{2,1,0:T(8,128)(2,1)S(1)} %collective-permute-done.9.refs_1_), channel_id=1, source_target_pairs={{0,2},{1,7},{2,4},{3,1},{4,6},{5,3},{6,0},{7,5},{8,10},{9,15},{10,... | collective-permute-start | bytes 2064392 | tf_op jit(solution)/shard_map/ppermute | solution.py:255
  67.2 28.1 %all-to-all-start.1 = ((s16[16,176,256]{2,1,0:T(8,128)(2,1)}), s16[16,176,256]{2,1,0:T(8,128)(2,1)}, u32[]{:S(2)}, u32[]{:S(2)}) async-start(s16[16,176,256]{2,1,0:T(8,128)(2,1)} %get-tuple-element.35), calls=%async_computation.1 | async-start | bytes 2883584 | tf_op jit(solution)/shard_map/all_to_all | solution.py:296
  71.6 2.7 %collective-permute-start.19 = (bf16[12,112,256]{2,1,0:T(8,128)(2,1)S(1)}, bf16[12,112,256]{2,1,0:T(8,128)(2,1)S(1)}, u32[]{:S(2)}, u32[]{:S(2)}) collective-permute-start(bf16[12,112,256]{2,1,0:T(8,128)(2,1)S(1)} %collective-permute-done.15.refs_2_), channel_id=1, source_target_pairs={{0,1},{1,0},{2,3},{3,2},{4,5},{5,4},{6,7},{7,6},{8,9},{9,8},{10,11... | collective-permute-start | bytes 2064392 | tf_op jit(solution)/shard_map/ppermute | solution.py:255
  71.7 4.1 %collective-permute-start.18 = (bf16[12,112,256]{2,1,0:T(8,128)(2,1)S(1)}, bf16[12,112,256]{2,1,0:T(8,128)(2,1)S(1)}, u32[]{:S(2)}, u32[]{:S(2)}) collective-permute-start(bf16[12,112,256]{2,1,0:T(8,128)(2,1)S(1)} %collective-permute-done.9.refs_1_), channel_id=1, source_target_pairs={{0,1},{1,0},{2,3},{3,2},{4,5},{5,4},{6,7},{7,6},{8,9},{9,8},{10,11... | collective-permute-start | bytes 2064392 | tf_op jit(solution)/shard_map/ppermute | solution.py:255
  72.2 3.6 %collective-permute-start.17 = (bf16[12,112,256]{2,1,0:T(8,128)(2,1)S(1)}, bf16[12,112,256]{2,1,0:T(8,128)(2,1)S(1)}, u32[]{:S(2)}, u32[]{:S(2)}) collective-permute-start(bf16[12,112,256]{2,1,0:T(8,128)(2,1)S(1)} %shard_map.64.refs_0_), channel_id=1, source_target_pairs={{0,1},{1,0},{2,3},{3,2},{4,5},{5,4},{6,7},{7,6},{8,9},{9,8},{10,11... | collective-permute-start | bytes 2064392 | tf_op jit(solution)/shard_map/ppermute | solution.py:255
  74.3 2.5 %collective-permute-start.20 = (bf16[12,112,256]{2,1,0:T(8,128)(2,1)S(1)}, bf16[12,112,256]{2,1,0:T(8,128)(2,1)S(1)}, u32[]{:S(2)}, u32[]{:S(2)}) collective-permute-start(bf16[12,112,256]{2,1,0:T(8,128)(2,1)S(1)} %collective-permute-done.16.refs_3_), channel_id=1, source_target_pairs={{0,1},{1,0},{2,3},{3,2},{4,5},{5,4},{6,7},{7,6},{8,9},{9,8},{10,11... | collective-permute-start | bytes 2064392 | tf_op jit(solution)/shard_map/ppermute | solution.py:255
  95.3 32.6 %all-to-all-start = ((s16[16,240,256]{2,1,0:T(8,128)(2,1)}), s16[16,240,256]{2,1,0:T(8,128)(2,1)S(1)}, u32[]{:S(2)}, u32[]{:S(2)}) async-start(s16[16,240,256]{2,1,0:T(8,128)(2,1)} %get-tuple-element.34), calls=%async_computation | async-start | bytes 3932160 | tf_op jit(solution)/shard_map/all_to_all | solution.py:296

commit v2 on v1

--- a/solution.py
+++ b/solution.py
@@ -10,7 +10,7 @@
 CAP = 2
 GROUPS = ((32,), (40,), (56,))
 META = 16
-LIMIT = 36 * 2**20
+LIMIT = 20 * 2**20
 STEPS = 32000.0
 MAGIC = 12582912.0
 TILE = 16
@@ -274,8 +274,8 @@
             x0, p1, p2 = near[i]
             if i > 0:
                 p1, x0, _ = tie(p1, x0, previous)
-            if i + 1 < n:
-                own[i + 1], p1 = tie(own[i + 1], p1)
+            if i == 0:
+                *own[1:], p1 = tie(*own[1:], p1)
             onward = move(p1, ahead)
             first = move(x0, swap)
             p1s, p2s = move(p1, swap), move(p2, swap)

time: 131 us -> 130 us (level)
  waiting for transfers between devices: 56.7 us -> 54.7 us
    ppermute x21, waiting for transfers between devices: 20.5 us -> 19.2 us  [move(): return lax.ppermute(v, 'int', perm)]
where the time goes in v2:
time: 130 us; the launch traced here: 129 us
  waiting for transfers between devices  54.7 us (42%)
  Pallas kernels  40.3 us (31%)
  starting transfers between devices  30.2 us (23%)
  local copies, waits for them, and re-layouts  3.26 us (3%)
    all_to_all x3, waiting for transfers between devices, body(): lax.all_to_all(sent[k], 'str', split_axis=0, concat_axis=0, tiled=True)  35.6 us
    pallas_call x3, Pallas kernels, product(): pl.pallas_call(functools.partial(product_kernel, base), grid_spec=grid, o...  28.2 us
    ppermute x21, waiting for transfers between devices, move(): return lax.ppermute(v, 'int', perm)  19.2 us
    all_to_all x3, starting transfers between devices, body(): lax.all_to_all(sent[k], 'str', split_axis=0, concat_axis=0, tiled=True)  16.4 us
    ppermute x21, starting transfers between devices, move(): return lax.ppermute(v, 'int', perm)  13.8 us
    pallas_call x3, Pallas kernels, add(): pl.pallas_call(functools.partial(add_kernel, places, n, far), in_specs=[h...  8.35 us
    pallas_call x3, Pallas kernels, split(): pl.pallas_call(functools.partial(split_kernel, r0), in_specs=[pl.BlockSpe...  3.67 us
    unnamed x23, local copies, waits for them, and re-layouts  3.17 us
  transfers between devices with their start and end apart: 24, of which 10 were waited for; matrix products, arithmetic and copies ran while one was open for 0% of the time, Pallas kernels for 28%

profile of v2, /device:TPU:0, one launch (start us, length us, event | category | flops | bytes accessed | tf_op | source)
XLA Modules:
  0.0 129.1 jit_solution(12433594990595418531)
XLA Ops:
  0.0 1.1 shard_map.66.refs_0_
  1.1 1.6 %collective-permute-start = (bf16[12,64,256]{2,1,0:T(8,128)(2,1)S(1)}, bf16[12,64,256]{2,1,0:T(8,128)(2,1)S(1)}, u32[]{:S(2)}, u32[]{:S(2)}) collective-permute-start(bf16[12,64,256]{2,1,0:T(8,128)(2,1)S(1)} %shard_map.66.refs_0_), channel_id=1, source_target_pairs={{0,2},{1,7},{2,4},{3,1},{4,6},{5,3},{6,0},{7,5},{8,10},{9,15},{10,... | collective-permute-start | bytes 1179656 | tf_op jit(solution)/shard_map/ppermute | solution.py:255
  2.8 1.7 %collective-permute-start.1 = (bf16[12,64,256]{2,1,0:T(8,128)(2,1)S(1)}, bf16[12,64,256]{2,1,0:T(8,128)(2,1)S(1)}, u32[]{:S(2)}, u32[]{:S(2)}) collective-permute-start(bf16[12,64,256]{2,1,0:T(8,128)(2,1)S(1)} %shard_map.66.refs_0_), channel_id=1, source_target_pairs={{0,6},{1,3},{2,0},{3,5},{4,2},{5,7},{6,4},{7,1},{8,14},{9,11},{10,... | collective-permute-start | bytes 1179656 | tf_op jit(solution)/shard_map/ppermute | solution.py:255
  4.4 1.2 shard_map.64.refs_0_
  5.6 0.0 copy-start.10
  5.7 0.0 copy-start.9
  5.7 0.0 copy-start.2
  5.7 0.0 copy-start.3
  5.7 1.3 %shard_map.65.refs_0_ = bf16[12,112,256]{2,1,0:T(8,128)(2,1)S(1)} custom-call(bf16[12,128,2,256]{3,2,1,0:T(2,128)(2,1)} %ci.5), custom_call_target="tpu_custom_call" | custom-call | tf_op jit(solution)/shard_map/pallas_call | solution.py:37
  7.0 5.9 %collective-permute-done.refs_1_ = bf16[12,64,256]{2,1,0:T(8,128)(2,1)S(1)} collective-permute-done((bf16[12,64,256]{2,1,0:T(8,128)(2,1)S(1)}, bf16[12,64,256]{2,1,0:T(8,128)(2,1)S(1)}, u32[]{:S(2)}, u32[]{:S(2)}) %collective-permute-start) | collective-permute-done | bytes 393248 | tf_op jit(solution)/shard_map/ppermute | solution.py:255
  12.9 1.7 %collective-permute-start.3 = (bf16[12,64,256]{2,1,0:T(8,128)(2,1)S(1)}, bf16[12,64,256]{2,1,0:T(8,128)(2,1)}, u32[]{:S(2)}, u32[]{:S(2)}) collective-permute-start(bf16[12,64,256]{2,1,0:T(8,128)(2,1)S(1)} %collective-permute-done.refs_1_), channel_id=1, source_target_pairs={{0,2},{1,7},{2,4},{3,1},{4,6},{5,3},{6,0},{7,5},{8,10},{9,15},{10,... | collective-permute-start | bytes 1179656 | tf_op jit(solution)/shard_map/ppermute | solution.py:255
  14.6 0.0 collective-permute-start.4
  14.6 0.0 collective-permute-done.1.refs_2_
  14.6 0.7 collective-permute-start.2
  15.4 1.0 collective-permute-start.5
  16.4 0.0 collective-permute-start.6
  16.4 5.6 %collective-permute-done.3.refs_3_ = bf16[12,64,256]{2,1,0:T(8,128)(2,1)} collective-permute-done((bf16[12,64,256]{2,1,0:T(8,128)(2,1)S(1)}, bf16[12,64,256]{2,1,0:T(8,128)(2,1)}, u32[]{:S(2)}, u32[]{:S(2)}) %collective-permute-start.3) | collective-permute-done | bytes 393248 | tf_op jit(solution)/shard_map/ppermute | solution.py:255
  22.0 0.0 collective-permute-start.7
  22.0 0.2 convert_reduce_fusion
  22.2 0.0 copy-start
  22.2 0.7 copy-done
  23.0 1.3 %collective-permute-start.8 = (bf16[12,80,256]{2,1,0:T(8,128)(2,1)S(1)}, bf16[12,80,256]{2,1,0:T(8,128)(2,1)S(1)}, u32[]{:S(2)}, u32[]{:S(2)}) collective-permute-start(bf16[12,80,256]{2,1,0:T(8,128)(2,1)S(1)} %shard_map.64.refs_0_), channel_id=1, source_target_pairs={{0,6},{1,3},{2,0},{3,5},{4,2},{5,7},{6,4},{7,1},{8,14},{9,11},{10,... | collective-permute-start | bytes 1474568 | tf_op jit(solution)/shard_map/ppermute | solution.py:255
  24.3 0.1 copy.10
  24.4 0.1 stack.35.place
  24.5 0.0 collective-permute-done.6.refs_6_
  24.5 0.0 collective-permute-done.5.refs_5_
  24.5 0.0 collective-permute-done.7.refs_7_
  24.5 0.0 copy-start.1
  24.5 1.0 copy-done.1
  25.5 8.5 %shard_map.67 = (f32[12,64,256]{2,1,0:T(8,128)}, s16[16,144,256]{2,1,0:T(8,128)(2,1)}) custom-call(s32[8]{0:T(128)S(1)} %stack.35.place, s32[12]{0:T(128)S(1)} %copy-done.2, s32[12]{0:T(128)S(1)} %multiply_add_fusion.slot, s32[12]{0:T(128)S(1)} %copy-done.3, f32[12,2]{1,0:T(8,128)S(1)} %convert_element_type.7.coef, ...), custom_call_target="tpu_custom_call" | custom-call | flops 1000000000 | bytes 10000 | tf_op jit(solution)/shard_map/pallas_call | solution.py:133
  34.0 0.0 collective-permute-done.2.refs_1_
  34.1 0.8 collective-permute-start.10
  34.8 8.3 %all-to-all-start.2 = ((s16[16,144,256]{2,1,0:T(8,128)(2,1)}), s16[16,144,256]{2,1,0:T(8,128)(2,1)}, u32[]{:S(2)}, u32[]{:S(2)}) async-start(s16[16,144,256]{2,1,0:T(8,128)(2,1)} %get-tuple-element.34), calls=%async_computation.2 | async-start | bytes 2359296 | tf_op jit(solution)/shard_map/all_to_all | solution.py:296
  43.1 0.0 collective-permute-done.8.refs_2_
  43.1 0.4 collective-permute-start.9
  43.5 0.7 collective-permute-start.13
  44.2 0.1 collective-permute-start.12
  44.3 0.4 collective-permute-start.11
  44.7 0.1 collective-permute-start.14
  44.8 0.9 collective-permute-done.13.refs_6_
  45.7 2.6 %collective-permute-start.15 = (bf16[12,112,256]{2,1,0:T(8,128)(2,1)S(1)}, bf16[12,112,256]{2,1,0:T(8,128)(2,1)S(1)}, u32[]{:S(2)}, u32[]{:S(2)}) collective-permute-start(bf16[12,112,256]{2,1,0:T(8,128)(2,1)S(1)} %shard_map.65.refs_0_), channel_id=1, source_target_pairs={{0,6},{1,3},{2,0},{3,5},{4,2},{5,7},{6,4},{7,1},{8,14},{9,11},{10,... | collective-permute-start | bytes 2064392 | tf_op jit(solution)/shard_map/ppermute | solution.py:255
  48.3 0.0 collective-permute-done.14.refs_7_
  48.3 0.0 copy-start.4
  48.3 0.6 copy-done.4
  49.0 0.7 copy-done.7
  49.6 8.9 %shard_map.68 = (f32[12,80,256]{2,1,0:T(8,128)}, s16[16,176,256]{2,1,0:T(8,128)(2,1)}) custom-call(s32[8]{0:T(128)S(1)} %stack.35.place, s32[12]{0:T(128)S(1)} %copy-done.2, s32[12]{0:T(128)S(1)} %copy-done.7, s32[12]{0:T(128)S(1)} %copy-done.4, f32[12,2]{1,0:T(8,128)S(1)} %convert_element_type.7.coef, bf16[12,80,256]{2,1,0:T(8,128)(2,1)S(1)} %shard_map.64.refs_0_, ...), custom_call_target="tpu_custom_call" | custom-call | flops 1000000000 | bytes 10000 | tf_op jit(solution)/shard_map/pallas_call | solution.py:133
  58.5 0.0 copy-start.5
  58.5 2.3 %collective-permute-done.9.refs_1_ = bf16[12,112,256]{2,1,0:T(8,128)(2,1)S(1)} collective-permute-done((bf16[12,112,256]{2,1,0:T(8,128)(2,1)S(1)}, bf16[12,112,256]{2,1,0:T(8,128)(2,1)S(1)}, u32[]{:S(2)}, u32[]{:S(2)}) %collective-permute-start.9) | collective-permute-done | bytes 688160 | tf_op jit(solution)/shard_map/ppermute | solution.py:255
  60.8 5.0 %all-to-all-done.2.refs_1_ = s16[16,144,256]{2,1,0:T(8,128)(2,1)} async-done(((s16[16,144,256]{2,1,0:T(8,128)(2,1)}), s16[16,144,256]{2,1,0:T(8,128)(2,1)}, u32[]{:S(2)}, u32[]{:S(2)}) %all-to-all-start.2) | async-done | bytes 1179680 | tf_op jit(solution)/shard_map/all_to_all | solution.py:296
  65.8 4.4 %all-to-all-start.1 = ((s16[16,176,256]{2,1,0:T(8,128)(2,1)}), s16[16,176,256]{2,1,0:T(8,128)(2,1)}, u32[]{:S(2)}, u32[]{:S(2)}) async-start(s16[16,176,256]{2,1,0:T(8,128)(2,1)} %get-tuple-element.33), calls=%async_computation.1 | async-start | bytes 2883584 | tf_op jit(solution)/shard_map/all_to_all | solution.py:296
  70.2 0.1 collective-permute-start.19
  70.3 0.5 collective-permute-start.18
  70.8 0.1 collective-permute-start.17
  70.9 2.0 %collective-permute-done.16.refs_3_ = bf16[12,112,256]{2,1,0:T(8,128)(2,1)S(1)} collective-permute-done((bf16[12,112,256]{2,1,0:T(8,128)(2,1)S(1)}, bf16[12,112,256]{2,1,0:T(8,128)(2,1)S(1)}, u32[]{:S(2)}, u32[]{:S(2)}) %collective-permute-start.16) | collective-permute-done | bytes 688160 | tf_op jit(solution)/shard_map/ppermute | solution.py:255
  72.9 0.0 collective-permute-start.20
  72.9 1.5 %collective-permute-done.17.refs_4_ = bf16[12,112,256]{2,1,0:T(8,128)(2,1)S(1)} collective-permute-done((bf16[12,112,256]{2,1,0:T(8,128)(2,1)S(1)}, bf16[12,112,256]{2,1,0:T(8,128)(2,1)S(1)}, u32[]{:S(2)}, u32[]{:S(2)}) %collective-permute-start.17) | collective-permute-done | bytes 688160 | tf_op jit(solution)/shard_map/ppermute | solution.py:255
  74.4 1.0 collective-permute-done.20.refs_7_
  75.4 10.9 %shard_map.69 = (f32[12,112,256]{2,1,0:T(8,128)}, s16[16,240,256]{2,1,0:T(8,128)(2,1)}) custom-call(s32[8]{0:T(128)S(1)} %stack.35.place, s32[12]{0:T(128)S(1)} %copy-done.2, s32[12]{0:T(128)S(1)} %copy-done.8, s32[12]{0:T(128)S(1)} %copy-done.5, f32[12,2]{1,0:T(8,128)S(1)} %convert_element_type.7.coef, bf16[12,112,256]{2,1,0:T(8,128)(2,1)S(1)} %shard_map.65.refs_0_, ...), custom_call_target="tpu_custom_call" | custom-call | flops 1000000000 | bytes 10000 | tf_op jit(solution)/shard_map/pallas_call | solution.py:133
  86.3 7.6 %all-to-all-done.1.refs_1_ = s16[16,176,256]{2,1,0:T(8,128)(2,1)} async-done(((s16[16,176,256]{2,1,0:T(8,128)(2,1)}), s16[16,176,256]{2,1,0:T(8,128)(2,1)}, u32[]{:S(2)}, u32[]{:S(2)}) %all-to-all-start.1) | async-done | bytes 1441824 | tf_op jit(solution)/shard_map/all_to_all | solution.py:296
  93.9 3.7 %all-to-all-start = ((s16[16,240,256]{2,1,0:T(8,128)(2,1)}), s16[16,240,256]{2,1,0:T(8,128)(2,1)S(1)}, u32[]{:S(2)}, u32[]{:S(2)}) async-start(s16[16,240,256]{2,1,0:T(8,128)(2,1)} %get-tuple-element.32), calls=%async_computation | async-start | bytes 3932160 | tf_op jit(solution)/shard_map/all_to_all | solution.py:296
  97.6 2.8 %shard_map.70.refs_2_ = bf16[12,128,2,256]{3,2,1,0:T(2,128)(2,1)} custom-call(f32[12,64,256]{2,1,0:T(8,128)} %get-tuple-element.24.refs_0_, s16[16,144,256]{2,1,0:T(8,128)(2,1)} %all-to-all-done.2.refs_1_), custom_call_target="tpu_custom_call" | custom-call | tf_op jit(solution)/shard_map/pallas_call | solution.py:209
  100.5 3.0 %shard_map.71.refs_2_ = bf16[12,128,2,256]{3,2,1,0:T(2,128)(2,1)} custom-call(f32[12,80,256]{2,1,0:T(8,128)} %get-tuple-element.28.refs_0_, s16[16,176,256]{2,1,0:T(8,128)(2,1)} %all-to-all-done.1.refs_1_, bf16[12,128,2,256]{3,2,1,0:T(2,128)(2,1)} %shard_map.70.refs_2_), custom_call_target="tpu_custom_call", output_to_operand_aliasing={{}: (2, {})} | custom-call | tf_op jit(solution)/shard_map/pallas_call | solution.py:209
  103.5 22.9 %all-to-all-done.refs_1_ = s16[16,240,256]{2,1,0:T(8,128)(2,1)S(1)} async-done(((s16[16,240,256]{2,1,0:T(8,128)(2,1)}), s16[16,240,256]{2,1,0:T(8,128)(2,1)S(1)}, u32[]{:S(2)}, u32[]{:S(2)}) %all-to-all-start) | async-done | bytes 1966112 | tf_op jit(solution)/shard_map/all_to_all | solution.py:296
  126.5 2.5 %shard_map.72 = bf16[12,128,2,256]{3,2,1,0:T(2,128)(2,1)} custom-call(f32[12,112,256]{2,1,0:T(8,128)} %get-tuple-element.31.refs_0_, s16[16,240,256]{2,1,0:T(8,128)(2,1)S(1)} %all-to-all-done.refs_1_, bf16[12,128,2,256]{3,2,1,0:T(2,128)(2,1)} %shard_map.71.refs_2_), custom_call_target="tpu_custom_call", output_to_operand_aliasing={{}: (2, {})} | custom-call | tf_op jit(solution)/shard_map/pallas_call | solution.py:209
  (20 shorter events, 0.1 us)
Async XLA Ops:
  1.1 11.8 %collective-permute-start = (bf16[12,64,256]{2,1,0:T(8,128)(2,1)S(1)}, bf16[12,64,256]{2,1,0:T(8,128)(2,1)S(1)}, u32[]{:S(2)}, u32[]{:S(2)}) collective-permute-start(bf16[12,64,256]{2,1,0:T(8,128)(2,1)S(1)} %shard_map.66.refs_0_), channel_id=1, source_target_pairs={{0,2},{1,7},{2,4},{3,1},{4,6},{5,3},{6,0},{7,5},{8,10},{9,15},{10,... | collective-permute-start | bytes 1179656 | tf_op jit(solution)/shard_map/ppermute | solution.py:255
  2.8 11.9 %collective-permute-start.1 = (bf16[12,64,256]{2,1,0:T(8,128)(2,1)S(1)}, bf16[12,64,256]{2,1,0:T(8,128)(2,1)S(1)}, u32[]{:S(2)}, u32[]{:S(2)}) collective-permute-start(bf16[12,64,256]{2,1,0:T(8,128)(2,1)S(1)} %shard_map.66.refs_0_), channel_id=1, source_target_pairs={{0,6},{1,3},{2,0},{3,5},{4,2},{5,7},{6,4},{7,1},{8,14},{9,11},{10,... | collective-permute-start | bytes 1179656 | tf_op jit(solution)/shard_map/ppermute | solution.py:255
  5.6 16.4 %copy-start.10 = (s32[12,1]{0,1:T(1,128)S(1)}, s32[12,1]{0,1:T(1,128)}, u32[]{:S(2)}) copy-start(s32[12,1]{0,1:T(1,128)} %param.9) | copy-start | bytes 148
  5.7 18.6 %copy-start.9 = (bf16[12,2]{0,1:T(2,128)(2,1)S(1)}, bf16[12,2]{0,1:T(2,128)(2,1)}, u32[]{:S(2)}) copy-start(bf16[12,2]{0,1:T(2,128)(2,1)} %param.11) | copy-start | bytes 148
  5.7 18.8 %copy-start.2 = (s32[12]{0:T(128)S(1)}, s32[12]{0:T(128)}, u32[]{:S(2)}) copy-start(s32[12]{0:T(128)} %sector.5) | copy-start | bytes 148
  5.7 18.8 %copy-start.3 = (s32[12]{0:T(128)S(1)}, s32[12]{0:T(128)}, u32[]{:S(2)}) copy-start(s32[12]{0:T(128)} %inner.5) | copy-start | bytes 148
  12.9 9.1 %collective-permute-start.3 = (bf16[12,64,256]{2,1,0:T(8,128)(2,1)S(1)}, bf16[12,64,256]{2,1,0:T(8,128)(2,1)}, u32[]{:S(2)}, u32[]{:S(2)}) collective-permute-start(bf16[12,64,256]{2,1,0:T(8,128)(2,1)S(1)} %collective-permute-done.refs_1_), channel_id=1, source_target_pairs={{0,2},{1,7},{2,4},{3,1},{4,6},{5,3},{6,0},{7,5},{8,10},{9,15},{10,... | collective-permute-start | bytes 1179656 | tf_op jit(solution)/shard_map/ppermute | solution.py:255
  14.6 7.6 %collective-permute-start.4 = (bf16[12,64,256]{2,1,0:T(8,128)(2,1)S(1)}, bf16[12,64,256]{2,1,0:T(8,128)(2,1)S(1)}, u32[]{:S(2)}, u32[]{:S(2)}) collective-permute-start(bf16[12,64,256]{2,1,0:T(8,128)(2,1)S(1)} %shard_map.66.refs_0_), channel_id=1, source_target_pairs={{0,1},{1,0},{2,3},{3,2},{4,5},{5,4},{6,7},{7,6},{8,9},{9,8},{10,11... | collective-permute-start | bytes 1179656 | tf_op jit(solution)/shard_map/ppermute | solution.py:255
  14.6 19.4 %collective-permute-start.2 = (bf16[12,80,256]{2,1,0:T(8,128)(2,1)S(1)}, bf16[12,80,256]{2,1,0:T(8,128)(2,1)S(1)}, u32[]{:S(2)}, u32[]{:S(2)}) collective-permute-start(bf16[12,80,256]{2,1,0:T(8,128)(2,1)S(1)} %shard_map.64.refs_0_), channel_id=1, source_target_pairs={{0,2},{1,7},{2,4},{3,1},{4,6},{5,3},{6,0},{7,5},{8,10},{9,15},{10,... | collective-permute-start | bytes 1474568 | tf_op jit(solution)/shard_map/ppermute | solution.py:255
  15.4 9.1 %collective-permute-start.5 = (bf16[12,64,256]{2,1,0:T(8,128)(2,1)S(1)}, bf16[12,64,256]{2,1,0:T(8,128)(2,1)}, u32[]{:S(2)}, u32[]{:S(2)}) collective-permute-start(bf16[12,64,256]{2,1,0:T(8,128)(2,1)S(1)} %collective-permute-done.refs_1_), channel_id=1, source_target_pairs={{0,1},{1,0},{2,3},{3,2},{4,5},{5,4},{6,7},{7,6},{8,9},{9,8},{10,11... | collective-permute-start | bytes 1179656 | tf_op jit(solution)/shard_map/ppermute | solution.py:255
  16.4 8.1 %collective-permute-start.6 = (bf16[12,64,256]{2,1,0:T(8,128)(2,1)S(1)}, bf16[12,64,256]{2,1,0:T(8,128)(2,1)}, u32[]{:S(2)}, u32[]{:S(2)}) collective-permute-start(bf16[12,64,256]{2,1,0:T(8,128)(2,1)S(1)} %collective-permute-done.1.refs_2_), channel_id=1, source_target_pairs={{0,1},{1,0},{2,3},{3,2},{4,5},{5,4},{6,7},{7,6},{8,9},{9,8},{10,11... | collective-permute-start | bytes 1179656 | tf_op jit(solution)/shard_map/ppermute | solution.py:255
  22.0 2.5 %collective-permute-start.7 = (bf16[12,64,256]{2,1,0:T(8,128)(2,1)}, bf16[12,64,256]{2,1,0:T(8,128)(2,1)}, u32[]{:S(2)}, u32[]{:S(2)}) collective-permute-start(bf16[12,64,256]{2,1,0:T(8,128)(2,1)} %collective-permute-done.3.refs_3_), channel_id=1, source_target_pairs={{0,1},{1,0},{2,3},{3,2},{4,5},{5,4},{6,7},{7,6},{8,9},{9,8},{10,11... | collective-permute-start | bytes 1179656 | tf_op jit(solution)/shard_map/ppermute | solution.py:255
  22.2 0.7 copy-start
  23.0 20.2 %collective-permute-start.8 = (bf16[12,80,256]{2,1,0:T(8,128)(2,1)S(1)}, bf16[12,80,256]{2,1,0:T(8,128)(2,1)S(1)}, u32[]{:S(2)}, u32[]{:S(2)}) collective-permute-start(bf16[12,80,256]{2,1,0:T(8,128)(2,1)S(1)} %shard_map.64.refs_0_), channel_id=1, source_target_pairs={{0,6},{1,3},{2,0},{3,5},{4,2},{5,7},{6,4},{7,1},{8,14},{9,11},{10,... | collective-permute-start | bytes 1474568 | tf_op jit(solution)/shard_map/ppermute | solution.py:255
  24.3 9.8 %copy-start.6 = (s32[12]{0:T(128)}, s32[12]{0:T(128)S(1)}, u32[]{:S(2)}) copy-start(s32[12]{0:T(128)S(1)} %multiply_add_fusion.slot) | copy-start | bytes 148
  24.5 1.0 copy-start.1
  34.1 10.6 %collective-permute-start.10 = (bf16[12,80,256]{2,1,0:T(8,128)(2,1)S(1)}, bf16[12,80,256]{2,1,0:T(8,128)(2,1)}, u32[]{:S(2)}, u32[]{:S(2)}) collective-permute-start(bf16[12,80,256]{2,1,0:T(8,128)(2,1)S(1)} %collective-permute-done.2.refs_1_), channel_id=1, source_target_pairs={{0,2},{1,7},{2,4},{3,1},{4,6},{5,3},{6,0},{7,5},{8,10},{9,15},{10,... | collective-permute-start | bytes 1474568 | tf_op jit(solution)/shard_map/ppermute | solution.py:255
  34.8 31.0 %all-to-all-start.2 = ((s16[16,144,256]{2,1,0:T(8,128)(2,1)}), s16[16,144,256]{2,1,0:T(8,128)(2,1)}, u32[]{:S(2)}, u32[]{:S(2)}) async-start(s16[16,144,256]{2,1,0:T(8,128)(2,1)} %get-tuple-element.34), calls=%async_computation.2 | async-start | bytes 2359296 | tf_op jit(solution)/shard_map/all_to_all | solution.py:296
  43.1 17.7 %collective-permute-start.9 = (bf16[12,112,256]{2,1,0:T(8,128)(2,1)S(1)}, bf16[12,112,256]{2,1,0:T(8,128)(2,1)S(1)}, u32[]{:S(2)}, u32[]{:S(2)}) collective-permute-start(bf16[12,112,256]{2,1,0:T(8,128)(2,1)S(1)} %shard_map.65.refs_0_), channel_id=1, source_target_pairs={{0,2},{1,7},{2,4},{3,1},{4,6},{5,3},{6,0},{7,5},{8,10},{9,15},{10,... | collective-permute-start | bytes 2064392 | tf_op jit(solution)/shard_map/ppermute | solution.py:255
  43.5 2.1 %collective-permute-start.13 = (bf16[12,80,256]{2,1,0:T(8,128)(2,1)S(1)}, bf16[12,80,256]{2,1,0:T(8,128)(2,1)S(1)}, u32[]{:S(2)}, u32[]{:S(2)}) collective-permute-start(bf16[12,80,256]{2,1,0:T(8,128)(2,1)S(1)} %collective-permute-done.8.refs_2_), channel_id=1, source_target_pairs={{0,1},{1,0},{2,3},{3,2},{4,5},{5,4},{6,7},{7,6},{8,9},{9,8},{10,11... | collective-permute-start | bytes 1474568 | tf_op jit(solution)/shard_map/ppermute | solution.py:255
  44.2 4.1 %collective-permute-start.12 = (bf16[12,80,256]{2,1,0:T(8,128)(2,1)S(1)}, bf16[12,80,256]{2,1,0:T(8,128)(2,1)S(1)}, u32[]{:S(2)}, u32[]{:S(2)}) collective-permute-start(bf16[12,80,256]{2,1,0:T(8,128)(2,1)S(1)} %collective-permute-done.2.refs_1_), channel_id=1, source_target_pairs={{0,1},{1,0},{2,3},{3,2},{4,5},{5,4},{6,7},{7,6},{8,9},{9,8},{10,11... | collective-permute-start | bytes 1474568 | tf_op jit(solution)/shard_map/ppermute | solution.py:255
  44.3 4.0 %collective-permute-start.11 = (bf16[12,80,256]{2,1,0:T(8,128)(2,1)S(1)}, bf16[12,80,256]{2,1,0:T(8,128)(2,1)S(1)}, u32[]{:S(2)}, u32[]{:S(2)}) collective-permute-start(bf16[12,80,256]{2,1,0:T(8,128)(2,1)S(1)} %shard_map.64.refs_0_), channel_id=1, source_target_pairs={{0,1},{1,0},{2,3},{3,2},{4,5},{5,4},{6,7},{7,6},{8,9},{9,8},{10,11... | collective-permute-start | bytes 1474568 | tf_op jit(solution)/shard_map/ppermute | solution.py:255
  44.7 3.6 %collective-permute-start.14 = (bf16[12,80,256]{2,1,0:T(8,128)(2,1)}, bf16[12,80,256]{2,1,0:T(8,128)(2,1)S(1)}, u32[]{:S(2)}, u32[]{:S(2)}) collective-permute-start(bf16[12,80,256]{2,1,0:T(8,128)(2,1)} %collective-permute-done.10.refs_3_), channel_id=1, source_target_pairs={{0,1},{1,0},{2,3},{3,2},{4,5},{5,4},{6,7},{7,6},{8,9},{9,8},{10,11... | collective-permute-start | bytes 1474568 | tf_op jit(solution)/shard_map/ppermute | solution.py:255
  45.7 24.6 %collective-permute-start.15 = (bf16[12,112,256]{2,1,0:T(8,128)(2,1)S(1)}, bf16[12,112,256]{2,1,0:T(8,128)(2,1)S(1)}, u32[]{:S(2)}, u32[]{:S(2)}) collective-permute-start(bf16[12,112,256]{2,1,0:T(8,128)(2,1)S(1)} %shard_map.65.refs_0_), channel_id=1, source_target_pairs={{0,6},{1,3},{2,0},{3,5},{4,2},{5,7},{6,4},{7,1},{8,14},{9,11},{10,... | collective-permute-start | bytes 2064392 | tf_op jit(solution)/shard_map/ppermute | solution.py:255
  48.3 0.7 copy-start.4
  49.0 0.7 copy-start.7
  58.5 16.9 %copy-start.5 = (s32[12]{0:T(128)S(1)}, s32[12]{0:T(128)}, u32[]{:S(2)}) copy-start(s32[12]{0:T(128)} %inner.5) | copy-start | bytes 148
  58.5 16.9 %copy-start.8 = (s32[12]{0:T(128)S(1)}, s32[12]{0:T(128)}, u32[]{:S(2)}) copy-start(s32[12]{0:T(128)} %copy-done.6) | copy-start | bytes 148
  60.8 12.1 %collective-permute-start.16 = (bf16[12,112,256]{2,1,0:T(8,128)(2,1)S(1)}, bf16[12,112,256]{2,1,0:T(8,128)(2,1)S(1)}, u32[]{:S(2)}, u32[]{:S(2)}) collective-permute-start(bf16[12,112,256]{2,1,0:T(8,128)(2,1)S(1)} %collective-permute-done.9.refs_1_), channel_id=1, source_target_pairs={{0,2},{1,7},{2,4},{3,1},{4,6},{5,3},{6,0},{7,5},{8,10},{9,15},{10,... | collective-permute-start | bytes 2064392 | tf_op jit(solution)/shard_map/ppermute | solution.py:255
  65.8 28.1 %all-to-all-start.1 = ((s16[16,176,256]{2,1,0:T(8,128)(2,1)}), s16[16,176,256]{2,1,0:T(8,128)(2,1)}, u32[]{:S(2)}, u32[]{:S(2)}) async-start(s16[16,176,256]{2,1,0:T(8,128)(2,1)} %get-tuple-element.33), calls=%async_computation.1 | async-start | bytes 2883584 | tf_op jit(solution)/shard_map/all_to_all | solution.py:296
  70.2 2.7 %collective-permute-start.19 = (bf16[12,112,256]{2,1,0:T(8,128)(2,1)S(1)}, bf16[12,112,256]{2,1,0:T(8,128)(2,1)S(1)}, u32[]{:S(2)}, u32[]{:S(2)}) collective-permute-start(bf16[12,112,256]{2,1,0:T(8,128)(2,1)S(1)} %collective-permute-done.15.refs_2_), channel_id=1, source_target_pairs={{0,1},{1,0},{2,3},{3,2},{4,5},{5,4},{6,7},{7,6},{8,9},{9,8},{10,11... | collective-permute-start | bytes 2064392 | tf_op jit(solution)/shard_map/ppermute | solution.py:255
  70.3 4.1 %collective-permute-start.18 = (bf16[12,112,256]{2,1,0:T(8,128)(2,1)S(1)}, bf16[12,112,256]{2,1,0:T(8,128)(2,1)S(1)}, u32[]{:S(2)}, u32[]{:S(2)}) collective-permute-start(bf16[12,112,256]{2,1,0:T(8,128)(2,1)S(1)} %collective-permute-done.9.refs_1_), channel_id=1, source_target_pairs={{0,1},{1,0},{2,3},{3,2},{4,5},{5,4},{6,7},{7,6},{8,9},{9,8},{10,11... | collective-permute-start | bytes 2064392 | tf_op jit(solution)/shard_map/ppermute | solution.py:255
  70.8 3.6 %collective-permute-start.17 = (bf16[12,112,256]{2,1,0:T(8,128)(2,1)S(1)}, bf16[12,112,256]{2,1,0:T(8,128)(2,1)S(1)}, u32[]{:S(2)}, u32[]{:S(2)}) collective-permute-start(bf16[12,112,256]{2,1,0:T(8,128)(2,1)S(1)} %shard_map.65.refs_0_), channel_id=1, source_target_pairs={{0,1},{1,0},{2,3},{3,2},{4,5},{5,4},{6,7},{7,6},{8,9},{9,8},{10,11... | collective-permute-start | bytes 2064392 | tf_op jit(solution)/shard_map/ppermute | solution.py:255
  72.9 2.5 %collective-permute-start.20 = (bf16[12,112,256]{2,1,0:T(8,128)(2,1)S(1)}, bf16[12,112,256]{2,1,0:T(8,128)(2,1)S(1)}, u32[]{:S(2)}, u32[]{:S(2)}) collective-permute-start(bf16[12,112,256]{2,1,0:T(8,128)(2,1)S(1)} %collective-permute-done.16.refs_3_), channel_id=1, source_target_pairs={{0,1},{1,0},{2,3},{3,2},{4,5},{5,4},{6,7},{7,6},{8,9},{9,8},{10,11... | collective-permute-start | bytes 2064392 | tf_op jit(solution)/shard_map/ppermute | solution.py:255
  93.9 32.6 %all-to-all-start = ((s16[16,240,256]{2,1,0:T(8,128)(2,1)}), s16[16,240,256]{2,1,0:T(8,128)(2,1)S(1)}, u32[]{:S(2)}, u32[]{:S(2)}) async-start(s16[16,240,256]{2,1,0:T(8,128)(2,1)} %get-tuple-element.32), calls=%async_computation | async-start | bytes 3932160 | tf_op jit(solution)/shard_map/all_to_all | solution.py:296

commit v3 on v2

--- a/solution.py
+++ b/solution.py
@@ -277,7 +277,8 @@
             if i == 0:
                 *own[1:], p1 = tie(*own[1:], p1)
             onward = move(p1, ahead)
-            first = move(x0, swap)
+            own_late, _ = tie(x0, onward)
+            first = move(own_late, swap)
             p1s, p2s = move(p1, swap), move(p2, swap)
             if i + 1 < n:
                 nxt, _, _ = tie(own[i + 1], p1, p2)

time: 130 us -> 128 us (0.985)
  waiting for transfers between devices: 54.7 us -> 52.9 us
    all_to_all x3, waiting for transfers between devices: 35.6 us -> 31.1 us  [body(): lax.all_to_all(sent[k], 'str', split_axis=0, concat_axis=0, tiled=True)]
    ppermute x21, waiting for transfers between devices: 19.2 us -> 21.9 us  [move(): return lax.ppermute(v, 'int', perm)]
  transfers between devices with their start and end apart: 24 -> 24, of which waited for: 10 -> 11; matrix products, arithmetic and copies ran while one was open for 0% -> 0% of each run, Pallas kernels for 28% -> 28%
where the time goes in v3:
time: 128 us
  waiting for transfers between devices  52.9 us (41%)
  Pallas kernels  39.6 us (31%)
  starting transfers between devices  31.2 us (24%)
  local copies, waits for them, and re-layouts  3.26 us (3%)
    all_to_all x3, waiting for transfers between devices, body(): lax.all_to_all(sent[k], 'str', split_axis=0, concat_axis=0, tiled=True)  31.1 us
    pallas_call x3, Pallas kernels, product(): pl.pallas_call(functools.partial(product_kernel, base), grid_spec=grid, o...  28.2 us
    ppermute x21, waiting for transfers between devices, move(): return lax.ppermute(v, 'int', perm)  21.9 us
    all_to_all x3, starting transfers between devices, body(): lax.all_to_all(sent[k], 'str', split_axis=0, concat_axis=0, tiled=True)  16.4 us
    ppermute x21, starting transfers between devices, move(): return lax.ppermute(v, 'int', perm)  14.8 us
    pallas_call x3, Pallas kernels, add(): pl.pallas_call(functools.partial(add_kernel, places, n, far), in_specs=[h...  7.75 us
    pallas_call x3, Pallas kernels, split(): pl.pallas_call(functools.partial(split_kernel, r0), in_specs=[pl.BlockSpe...  3.67 us
    unnamed x23, local copies, waits for them, and re-layouts  3.17 us
  transfers between devices with their start and end apart: 24, of which 11 were waited for; matrix products, arithmetic and copies ran while one was open for 0% of the time, Pallas kernels for 28%

profile of v3, /device:TPU:0, one launch (start us, length us, event | category | flops | bytes accessed | tf_op | source)
XLA Modules:
  0.0 127.6 jit_solution(6218807098445790256)
XLA Ops:
  0.0 1.1 shard_map.66.refs_0_
  1.1 1.6 %collective-permute-start = (bf16[12,64,256]{2,1,0:T(8,128)(2,1)S(1)}, bf16[12,64,256]{2,1,0:T(8,128)(2,1)S(1)}, u32[]{:S(2)}, u32[]{:S(2)}) collective-permute-start(bf16[12,64,256]{2,1,0:T(8,128)(2,1)S(1)} %shard_map.66.refs_0_), channel_id=1, source_target_pairs={{0,2},{1,7},{2,4},{3,1},{4,6},{5,3},{6,0},{7,5},{8,10},{9,15},{10,... | collective-permute-start | bytes 1179656 | tf_op jit(solution)/shard_map/ppermute | solution.py:255
  2.8 1.7 %collective-permute-start.1 = (bf16[12,64,256]{2,1,0:T(8,128)(2,1)S(1)}, bf16[12,64,256]{2,1,0:T(8,128)(2,1)S(1)}, u32[]{:S(2)}, u32[]{:S(2)}) collective-permute-start(bf16[12,64,256]{2,1,0:T(8,128)(2,1)S(1)} %shard_map.66.refs_0_), channel_id=1, source_target_pairs={{0,6},{1,3},{2,0},{3,5},{4,2},{5,7},{6,4},{7,1},{8,14},{9,11},{10,... | collective-permute-start | bytes 1179656 | tf_op jit(solution)/shard_map/ppermute | solution.py:255
  4.4 1.2 shard_map.64.refs_0_
  5.6 0.0 copy-start.10
  5.7 0.0 copy-start.9
  5.7 0.0 copy-start.2
  5.7 0.0 copy-start.3
  5.7 1.3 %shard_map.65.refs_0_ = bf16[12,112,256]{2,1,0:T(8,128)(2,1)S(1)} custom-call(bf16[12,128,2,256]{3,2,1,0:T(2,128)(2,1)} %ci.5), custom_call_target="tpu_custom_call" | custom-call | tf_op jit(solution)/shard_map/pallas_call | solution.py:37
  7.0 5.9 %collective-permute-done.refs_1_ = bf16[12,64,256]{2,1,0:T(8,128)(2,1)S(1)} collective-permute-done((bf16[12,64,256]{2,1,0:T(8,128)(2,1)S(1)}, bf16[12,64,256]{2,1,0:T(8,128)(2,1)S(1)}, u32[]{:S(2)}, u32[]{:S(2)}) %collective-permute-start) | collective-permute-done | bytes 393248 | tf_op jit(solution)/shard_map/ppermute | solution.py:255
  12.9 1.7 %collective-permute-start.3 = (bf16[12,64,256]{2,1,0:T(8,128)(2,1)S(1)}, bf16[12,64,256]{2,1,0:T(8,128)(2,1)}, u32[]{:S(2)}, u32[]{:S(2)}) collective-permute-start(bf16[12,64,256]{2,1,0:T(8,128)(2,1)S(1)} %collective-permute-done.refs_1_), channel_id=1, source_target_pairs={{0,2},{1,7},{2,4},{3,1},{4,6},{5,3},{6,0},{7,5},{8,10},{9,15},{10,... | collective-permute-start | bytes 1179656 | tf_op jit(solution)/shard_map/ppermute | solution.py:255
  14.6 0.0 collective-permute-done.1.refs_2_
  14.6 0.0 collective-permute-start.6
  14.6 0.7 collective-permute-start.2
  15.4 1.0 collective-permute-start.5
  16.4 5.6 %collective-permute-done.3.refs_3_ = bf16[12,64,256]{2,1,0:T(8,128)(2,1)} collective-permute-done((bf16[12,64,256]{2,1,0:T(8,128)(2,1)S(1)}, bf16[12,64,256]{2,1,0:T(8,128)(2,1)}, u32[]{:S(2)}, u32[]{:S(2)}) %collective-permute-start.3) | collective-permute-done | bytes 393248 | tf_op jit(solution)/shard_map/ppermute | solution.py:255
  22.0 0.0 collective-permute-start.4
  22.0 0.5 collective-permute-start.7
  22.5 0.2 convert_reduce_fusion
  22.7 0.0 collective-permute-done.6.refs_6_
  22.7 0.0 copy-start
  22.7 0.7 copy-done
  23.5 1.3 %collective-permute-start.8 = (bf16[12,80,256]{2,1,0:T(8,128)(2,1)S(1)}, bf16[12,80,256]{2,1,0:T(8,128)(2,1)S(1)}, u32[]{:S(2)}, u32[]{:S(2)}) collective-permute-start(bf16[12,80,256]{2,1,0:T(8,128)(2,1)S(1)} %shard_map.64.refs_0_), channel_id=1, source_target_pairs={{0,6},{1,3},{2,0},{3,5},{4,2},{5,7},{6,4},{7,1},{8,14},{9,11},{10,... | collective-permute-start | bytes 1474568 | tf_op jit(solution)/shard_map/ppermute | solution.py:255
  24.8 0.1 copy.10
  24.9 0.1 stack.35.place
  25.0 0.0 collective-permute-done.5.refs_5_
  25.0 0.0 collective-permute-done.4.refs_4_
  25.0 0.0 copy-start.1
  25.0 1.0 copy-done.1
  26.0 8.5 %shard_map.67 = (f32[12,64,256]{2,1,0:T(8,128)}, s16[16,144,256]{2,1,0:T(8,128)(2,1)}) custom-call(s32[8]{0:T(128)S(1)} %stack.35.place, s32[12]{0:T(128)S(1)} %copy-done.2, s32[12]{0:T(128)S(1)} %multiply_add_fusion.slot, s32[12]{0:T(128)S(1)} %copy-done.3, f32[12,2]{1,0:T(8,128)S(1)} %convert_element_type.7.coef, ...), custom_call_target="tpu_custom_call" | custom-call | flops 1000000000 | bytes 10000 | tf_op jit(solution)/shard_map/pallas_call | solution.py:133
  34.5 0.8 collective-permute-start.10
  35.3 8.3 %all-to-all-start.2 = ((s16[16,144,256]{2,1,0:T(8,128)(2,1)}), s16[16,144,256]{2,1,0:T(8,128)(2,1)}, u32[]{:S(2)}, u32[]{:S(2)}) async-start(s16[16,144,256]{2,1,0:T(8,128)(2,1)} %get-tuple-element.40), calls=%async_computation.2 | async-start | bytes 2359296 | tf_op jit(solution)/shard_map/all_to_all | solution.py:297
  43.6 0.4 collective-permute-start.9
  44.0 0.1 collective-permute-start.13
  44.2 0.4 collective-permute-start.12
  44.5 0.2 collective-permute-done.10.refs_3_
  44.8 0.0 collective-permute-start.11
  44.8 0.5 collective-permute-start.14
  45.3 0.6 collective-permute-done.13.refs_6_
  45.9 2.9 %collective-permute-start.15 = (bf16[12,112,256]{2,1,0:T(8,128)(2,1)S(1)}, bf16[12,112,256]{2,1,0:T(8,128)(2,1)S(1)}, u32[]{:S(2)}, u32[]{:S(2)}) collective-permute-start(bf16[12,112,256]{2,1,0:T(8,128)(2,1)S(1)} %shard_map.65.refs_0_), channel_id=1, source_target_pairs={{0,6},{1,3},{2,0},{3,5},{4,2},{5,7},{6,4},{7,1},{8,14},{9,11},{10,... | collective-permute-start | bytes 2064392 | tf_op jit(solution)/shard_map/ppermute | solution.py:255
  48.8 0.0 collective-permute-done.12.refs_5_
  48.8 0.0 collective-permute-done.11.refs_4_
  48.8 0.0 collective-permute-done.14.refs_7_
  48.8 0.0 copy-start.4
  48.8 0.6 copy-done.4
  49.5 0.7 copy-done.7
  50.1 8.9 %shard_map.68 = (f32[12,80,256]{2,1,0:T(8,128)}, s16[16,176,256]{2,1,0:T(8,128)(2,1)}) custom-call(s32[8]{0:T(128)S(1)} %stack.35.place, s32[12]{0:T(128)S(1)} %copy-done.2, s32[12]{0:T(128)S(1)} %copy-done.7, s32[12]{0:T(128)S(1)} %copy-done.4, f32[12,2]{1,0:T(8,128)S(1)} %convert_element_type.7.coef, bf16[12,80,256]{2,1,0:T(8,128)(2,1)S(1)} %shard_map.64.refs_0_, ...), custom_call_target="tpu_custom_call" | custom-call | flops 1000000000 | bytes 10000 | tf_op jit(solution)/shard_map/pallas_call | solution.py:133
  59.0 0.0 copy-start.5
  59.0 2.8 %collective-permute-done.9.refs_1_ = bf16[12,112,256]{2,1,0:T(8,128)(2,1)S(1)} collective-permute-done((bf16[12,112,256]{2,1,0:T(8,128)(2,1)S(1)}, bf16[12,112,256]{2,1,0:T(8,128)(2,1)S(1)}, u32[]{:S(2)}, u32[]{:S(2)}) %collective-permute-start.9) | collective-permute-done | bytes 688160 | tf_op jit(solution)/shard_map/ppermute | solution.py:255
  61.8 3.1 %all-to-all-done.2.refs_1_ = s16[16,144,256]{2,1,0:T(8,128)(2,1)} async-done(((s16[16,144,256]{2,1,0:T(8,128)(2,1)}), s16[16,144,256]{2,1,0:T(8,128)(2,1)}, u32[]{:S(2)}, u32[]{:S(2)}) %all-to-all-start.2) | async-done | bytes 1179680 | tf_op jit(solution)/shard_map/all_to_all | solution.py:297
  64.9 4.4 %all-to-all-start.1 = ((s16[16,176,256]{2,1,0:T(8,128)(2,1)}), s16[16,176,256]{2,1,0:T(8,128)(2,1)}, u32[]{:S(2)}, u32[]{:S(2)}) async-start(s16[16,176,256]{2,1,0:T(8,128)(2,1)} %get-tuple-element.39), calls=%async_computation.1 | async-start | bytes 2883584 | tf_op jit(solution)/shard_map/all_to_all | solution.py:297
  69.3 0.1 collective-permute-start.19
  69.4 0.5 collective-permute-start.18
  69.9 4.1 %collective-permute-done.16.refs_3_ = bf16[12,112,256]{2,1,0:T(8,128)(2,1)S(1)} collective-permute-done((bf16[12,112,256]{2,1,0:T(8,128)(2,1)S(1)}, bf16[12,112,256]{2,1,0:T(8,128)(2,1)S(1)}, u32[]{:S(2)}, u32[]{:S(2)}) %collective-permute-start.16) | collective-permute-done | bytes 688160 | tf_op jit(solution)/shard_map/ppermute | solution.py:255
  73.9 0.5 collective-permute-start.20
  74.5 1.6 %collective-permute-done.17.refs_4_ = bf16[12,112,256]{2,1,0:T(8,128)(2,1)S(1)} collective-permute-done((bf16[12,112,256]{2,1,0:T(8,128)(2,1)S(1)}, bf16[12,112,256]{2,1,0:T(8,128)(2,1)S(1)}, u32[]{:S(2)}, u32[]{:S(2)}) %collective-permute-start.17) | collective-permute-done | bytes 688160 | tf_op jit(solution)/shard_map/ppermute | solution.py:255
  76.1 1.0 collective-permute-done.20.refs_7_
  77.1 10.9 %shard_map.69 = (f32[12,112,256]{2,1,0:T(8,128)}, s16[16,240,256]{2,1,0:T(8,128)(2,1)}) custom-call(s32[8]{0:T(128)S(1)} %stack.35.place, s32[12]{0:T(128)S(1)} %copy-done.2, s32[12]{0:T(128)S(1)} %copy-done.8, s32[12]{0:T(128)S(1)} %copy-done.5, f32[12,2]{1,0:T(8,128)S(1)} %convert_element_type.7.coef, bf16[12,112,256]{2,1,0:T(8,128)(2,1)S(1)} %shard_map.65.refs_0_, ...), custom_call_target="tpu_custom_call" | custom-call | flops 1000000000 | bytes 10000 | tf_op jit(solution)/shard_map/pallas_call | solution.py:133
  88.0 4.0 %all-to-all-done.1.refs_1_ = s16[16,176,256]{2,1,0:T(8,128)(2,1)} async-done(((s16[16,176,256]{2,1,0:T(8,128)(2,1)}), s16[16,176,256]{2,1,0:T(8,128)(2,1)}, u32[]{:S(2)}, u32[]{:S(2)}) %all-to-all-start.1) | async-done | bytes 1441824 | tf_op jit(solution)/shard_map/all_to_all | solution.py:297
  92.0 3.7 %all-to-all-start = ((s16[16,240,256]{2,1,0:T(8,128)(2,1)}), s16[16,240,256]{2,1,0:T(8,128)(2,1)S(1)}, u32[]{:S(2)}, u32[]{:S(2)}) async-start(s16[16,240,256]{2,1,0:T(8,128)(2,1)} %get-tuple-element.38), calls=%async_computation | async-start | bytes 3932160 | tf_op jit(solution)/shard_map/all_to_all | solution.py:297
  95.7 2.6 %shard_map.70.refs_2_ = bf16[12,128,2,256]{3,2,1,0:T(2,128)(2,1)} custom-call(f32[12,64,256]{2,1,0:T(8,128)} %get-tuple-element.28.refs_0_, s16[16,144,256]{2,1,0:T(8,128)(2,1)} %all-to-all-done.2.refs_1_), custom_call_target="tpu_custom_call" | custom-call | tf_op jit(solution)/shard_map/pallas_call | solution.py:209
  98.3 2.7 %shard_map.71.refs_2_ = bf16[12,128,2,256]{3,2,1,0:T(2,128)(2,1)} custom-call(f32[12,80,256]{2,1,0:T(8,128)} %get-tuple-element.33.refs_0_, s16[16,176,256]{2,1,0:T(8,128)(2,1)} %all-to-all-done.1.refs_1_, bf16[12,128,2,256]{3,2,1,0:T(2,128)(2,1)} %shard_map.70.refs_2_), custom_call_target="tpu_custom_call", output_to_operand_aliasing={{}: (2, {})} | custom-call | tf_op jit(solution)/shard_map/pallas_call | solution.py:209
  101.0 24.0 %all-to-all-done.refs_1_ = s16[16,240,256]{2,1,0:T(8,128)(2,1)S(1)} async-done(((s16[16,240,256]{2,1,0:T(8,128)(2,1)}), s16[16,240,256]{2,1,0:T(8,128)(2,1)S(1)}, u32[]{:S(2)}, u32[]{:S(2)}) %all-to-all-start) | async-done | bytes 1966112 | tf_op jit(solution)/shard_map/all_to_all | solution.py:297
  125.0 2.5 %shard_map.72 = bf16[12,128,2,256]{3,2,1,0:T(2,128)(2,1)} custom-call(f32[12,112,256]{2,1,0:T(8,128)} %get-tuple-element.37.refs_0_, s16[16,240,256]{2,1,0:T(8,128)(2,1)S(1)} %all-to-all-done.refs_1_, bf16[12,128,2,256]{3,2,1,0:T(2,128)(2,1)} %shard_map.71.refs_2_), custom_call_target="tpu_custom_call", output_to_operand_aliasing={{}: (2, {})} | custom-call | tf_op jit(solution)/shard_map/pallas_call | solution.py:209
  (20 shorter events, 0.1 us)
Async XLA Ops:
  1.1 11.8 %collective-permute-start = (bf16[12,64,256]{2,1,0:T(8,128)(2,1)S(1)}, bf16[12,64,256]{2,1,0:T(8,128)(2,1)S(1)}, u32[]{:S(2)}, u32[]{:S(2)}) collective-permute-start(bf16[12,64,256]{2,1,0:T(8,128)(2,1)S(1)} %shard_map.66.refs_0_), channel_id=1, source_target_pairs={{0,2},{1,7},{2,4},{3,1},{4,6},{5,3},{6,0},{7,5},{8,10},{9,15},{10,... | collective-permute-start | bytes 1179656 | tf_op jit(solution)/shard_map/ppermute | solution.py:255
  2.8 11.9 %collective-permute-start.1 = (bf16[12,64,256]{2,1,0:T(8,128)(2,1)S(1)}, bf16[12,64,256]{2,1,0:T(8,128)(2,1)S(1)}, u32[]{:S(2)}, u32[]{:S(2)}) collective-permute-start(bf16[12,64,256]{2,1,0:T(8,128)(2,1)S(1)} %shard_map.66.refs_0_), channel_id=1, source_target_pairs={{0,6},{1,3},{2,0},{3,5},{4,2},{5,7},{6,4},{7,1},{8,14},{9,11},{10,... | collective-permute-start | bytes 1179656 | tf_op jit(solution)/shard_map/ppermute | solution.py:255
  5.6 16.9 %copy-start.10 = (s32[12,1]{0,1:T(1,128)S(1)}, s32[12,1]{0,1:T(1,128)}, u32[]{:S(2)}) copy-start(s32[12,1]{0,1:T(1,128)} %param.9) | copy-start | bytes 148
  5.7 19.1 %copy-start.9 = (bf16[12,2]{0,1:T(2,128)(2,1)S(1)}, bf16[12,2]{0,1:T(2,128)(2,1)}, u32[]{:S(2)}) copy-start(bf16[12,2]{0,1:T(2,128)(2,1)} %param.11) | copy-start | bytes 148
  5.7 19.3 %copy-start.2 = (s32[12]{0:T(128)S(1)}, s32[12]{0:T(128)}, u32[]{:S(2)}) copy-start(s32[12]{0:T(128)} %sector.5) | copy-start | bytes 148
  5.7 19.3 %copy-start.3 = (s32[12]{0:T(128)S(1)}, s32[12]{0:T(128)}, u32[]{:S(2)}) copy-start(s32[12]{0:T(128)} %inner.5) | copy-start | bytes 148
  12.9 9.1 %collective-permute-start.3 = (bf16[12,64,256]{2,1,0:T(8,128)(2,1)S(1)}, bf16[12,64,256]{2,1,0:T(8,128)(2,1)}, u32[]{:S(2)}, u32[]{:S(2)}) collective-permute-start(bf16[12,64,256]{2,1,0:T(8,128)(2,1)S(1)} %collective-permute-done.refs_1_), channel_id=1, source_target_pairs={{0,2},{1,7},{2,4},{3,1},{4,6},{5,3},{6,0},{7,5},{8,10},{9,15},{10,... | collective-permute-start | bytes 1179656 | tf_op jit(solution)/shard_map/ppermute | solution.py:255
  14.6 8.1 %collective-permute-start.6 = (bf16[12,64,256]{2,1,0:T(8,128)(2,1)S(1)}, bf16[12,64,256]{2,1,0:T(8,128)(2,1)S(1)}, u32[]{:S(2)}, u32[]{:S(2)}) collective-permute-start(bf16[12,64,256]{2,1,0:T(8,128)(2,1)S(1)} %collective-permute-done.1.refs_2_), channel_id=1, source_target_pairs={{0,1},{1,0},{2,3},{3,2},{4,5},{5,4},{6,7},{7,6},{8,9},{9,8},{10,11... | collective-permute-start | bytes 1179656 | tf_op jit(solution)/shard_map/ppermute | solution.py:255
  14.6 19.9 %collective-permute-start.2 = (bf16[12,80,256]{2,1,0:T(8,128)(2,1)S(1)}, bf16[12,80,256]{2,1,0:T(8,128)(2,1)S(1)}, u32[]{:S(2)}, u32[]{:S(2)}) collective-permute-start(bf16[12,80,256]{2,1,0:T(8,128)(2,1)S(1)} %shard_map.64.refs_0_), channel_id=1, source_target_pairs={{0,2},{1,7},{2,4},{3,1},{4,6},{5,3},{6,0},{7,5},{8,10},{9,15},{10,... | collective-permute-start | bytes 1474568 | tf_op jit(solution)/shard_map/ppermute | solution.py:255
  15.4 9.6 %collective-permute-start.5 = (bf16[12,64,256]{2,1,0:T(8,128)(2,1)S(1)}, bf16[12,64,256]{2,1,0:T(8,128)(2,1)}, u32[]{:S(2)}, u32[]{:S(2)}) collective-permute-start(bf16[12,64,256]{2,1,0:T(8,128)(2,1)S(1)} %collective-permute-done.refs_1_), channel_id=1, source_target_pairs={{0,1},{1,0},{2,3},{3,2},{4,5},{5,4},{6,7},{7,6},{8,9},{9,8},{10,11... | collective-permute-start | bytes 1179656 | tf_op jit(solution)/shard_map/ppermute | solution.py:255
  22.0 3.0 %collective-permute-start.4 = (bf16[12,64,256]{2,1,0:T(8,128)(2,1)S(1)}, bf16[12,64,256]{2,1,0:T(8,128)(2,1)}, u32[]{:S(2)}, u32[]{:S(2)}) collective-permute-start(bf16[12,64,256]{2,1,0:T(8,128)(2,1)S(1)} %shard_map.66.refs_0_), channel_id=1, source_target_pairs={{0,1},{1,0},{2,3},{3,2},{4,5},{5,4},{6,7},{7,6},{8,9},{9,8},{10,11... | collective-permute-start | bytes 1179656 | tf_op jit(solution)/shard_map/ppermute | solution.py:255
  22.0 3.0 %collective-permute-start.7 = (bf16[12,64,256]{2,1,0:T(8,128)(2,1)}, bf16[12,64,256]{2,1,0:T(8,128)(2,1)}, u32[]{:S(2)}, u32[]{:S(2)}) collective-permute-start(bf16[12,64,256]{2,1,0:T(8,128)(2,1)} %collective-permute-done.3.refs_3_), channel_id=1, source_target_pairs={{0,1},{1,0},{2,3},{3,2},{4,5},{5,4},{6,7},{7,6},{8,9},{9,8},{10,11... | collective-permute-start | bytes 1179656 | tf_op jit(solution)/shard_map/ppermute | solution.py:255
  22.7 0.7 copy-start
  23.5 20.1 %collective-permute-start.8 = (bf16[12,80,256]{2,1,0:T(8,128)(2,1)S(1)}, bf16[12,80,256]{2,1,0:T(8,128)(2,1)S(1)}, u32[]{:S(2)}, u32[]{:S(2)}) collective-permute-start(bf16[12,80,256]{2,1,0:T(8,128)(2,1)S(1)} %shard_map.64.refs_0_), channel_id=1, source_target_pairs={{0,6},{1,3},{2,0},{3,5},{4,2},{5,7},{6,4},{7,1},{8,14},{9,11},{10,... | collective-permute-start | bytes 1474568 | tf_op jit(solution)/shard_map/ppermute | solution.py:255
  24.8 9.7 %copy-start.6 = (s32[12]{0:T(128)}, s32[12]{0:T(128)S(1)}, u32[]{:S(2)}) copy-start(s32[12]{0:T(128)S(1)} %multiply_add_fusion.slot) | copy-start | bytes 148
  25.0 1.0 copy-start.1
  34.5 10.2 %collective-permute-start.10 = (bf16[12,80,256]{2,1,0:T(8,128)(2,1)S(1)}, bf16[12,80,256]{2,1,0:T(8,128)(2,1)}, u32[]{:S(2)}, u32[]{:S(2)}) collective-permute-start(bf16[12,80,256]{2,1,0:T(8,128)(2,1)S(1)} %collective-permute-done.2.refs_1_), channel_id=1, source_target_pairs={{0,2},{1,7},{2,4},{3,1},{4,6},{5,3},{6,0},{7,5},{8,10},{9,15},{10,... | collective-permute-start | bytes 1474568 | tf_op jit(solution)/shard_map/ppermute | solution.py:255
  35.3 29.5 %all-to-all-start.2 = ((s16[16,144,256]{2,1,0:T(8,128)(2,1)}), s16[16,144,256]{2,1,0:T(8,128)(2,1)}, u32[]{:S(2)}, u32[]{:S(2)}) async-start(s16[16,144,256]{2,1,0:T(8,128)(2,1)} %get-tuple-element.40), calls=%async_computation.2 | async-start | bytes 2359296 | tf_op jit(solution)/shard_map/all_to_all | solution.py:297
  43.6 18.2 %collective-permute-start.9 = (bf16[12,112,256]{2,1,0:T(8,128)(2,1)S(1)}, bf16[12,112,256]{2,1,0:T(8,128)(2,1)S(1)}, u32[]{:S(2)}, u32[]{:S(2)}) collective-permute-start(bf16[12,112,256]{2,1,0:T(8,128)(2,1)S(1)} %shard_map.65.refs_0_), channel_id=1, source_target_pairs={{0,2},{1,7},{2,4},{3,1},{4,6},{5,3},{6,0},{7,5},{8,10},{9,15},{10,... | collective-permute-start | bytes 2064392 | tf_op jit(solution)/shard_map/ppermute | solution.py:255
  44.0 1.9 %collective-permute-start.13 = (bf16[12,80,256]{2,1,0:T(8,128)(2,1)S(1)}, bf16[12,80,256]{2,1,0:T(8,128)(2,1)S(1)}, u32[]{:S(2)}, u32[]{:S(2)}) collective-permute-start(bf16[12,80,256]{2,1,0:T(8,128)(2,1)S(1)} %collective-permute-done.8.refs_2_), channel_id=1, source_target_pairs={{0,1},{1,0},{2,3},{3,2},{4,5},{5,4},{6,7},{7,6},{8,9},{9,8},{10,11... | collective-permute-start | bytes 1474568 | tf_op jit(solution)/shard_map/ppermute | solution.py:255
  44.2 4.6 %collective-permute-start.12 = (bf16[12,80,256]{2,1,0:T(8,128)(2,1)S(1)}, bf16[12,80,256]{2,1,0:T(8,128)(2,1)S(1)}, u32[]{:S(2)}, u32[]{:S(2)}) collective-permute-start(bf16[12,80,256]{2,1,0:T(8,128)(2,1)S(1)} %collective-permute-done.2.refs_1_), channel_id=1, source_target_pairs={{0,1},{1,0},{2,3},{3,2},{4,5},{5,4},{6,7},{7,6},{8,9},{9,8},{10,11... | collective-permute-start | bytes 1474568 | tf_op jit(solution)/shard_map/ppermute | solution.py:255
  44.8 4.0 %collective-permute-start.11 = (bf16[12,80,256]{2,1,0:T(8,128)(2,1)S(1)}, bf16[12,80,256]{2,1,0:T(8,128)(2,1)S(1)}, u32[]{:S(2)}, u32[]{:S(2)}) collective-permute-start(bf16[12,80,256]{2,1,0:T(8,128)(2,1)S(1)} %shard_map.64.refs_0_), channel_id=1, source_target_pairs={{0,1},{1,0},{2,3},{3,2},{4,5},{5,4},{6,7},{7,6},{8,9},{9,8},{10,11... | collective-permute-start | bytes 1474568 | tf_op jit(solution)/shard_map/ppermute | solution.py:255
  44.8 4.0 %collective-permute-start.14 = (bf16[12,80,256]{2,1,0:T(8,128)(2,1)}, bf16[12,80,256]{2,1,0:T(8,128)(2,1)S(1)}, u32[]{:S(2)}, u32[]{:S(2)}) collective-permute-start(bf16[12,80,256]{2,1,0:T(8,128)(2,1)} %collective-permute-done.10.refs_3_), channel_id=1, source_target_pairs={{0,1},{1,0},{2,3},{3,2},{4,5},{5,4},{6,7},{7,6},{8,9},{9,8},{10,11... | collective-permute-start | bytes 1474568 | tf_op jit(solution)/shard_map/ppermute | solution.py:255
  45.9 23.4 %collective-permute-start.15 = (bf16[12,112,256]{2,1,0:T(8,128)(2,1)S(1)}, bf16[12,112,256]{2,1,0:T(8,128)(2,1)S(1)}, u32[]{:S(2)}, u32[]{:S(2)}) collective-permute-start(bf16[12,112,256]{2,1,0:T(8,128)(2,1)S(1)} %shard_map.65.refs_0_), channel_id=1, source_target_pairs={{0,6},{1,3},{2,0},{3,5},{4,2},{5,7},{6,4},{7,1},{8,14},{9,11},{10,... | collective-permute-start | bytes 2064392 | tf_op jit(solution)/shard_map/ppermute | solution.py:255
  48.8 0.7 copy-start.4
  49.5 0.7 copy-start.7
  59.0 18.1 %copy-start.5 = (s32[12]{0:T(128)S(1)}, s32[12]{0:T(128)}, u32[]{:S(2)}) copy-start(s32[12]{0:T(128)} %inner.5) | copy-start | bytes 148
  59.0 18.1 %copy-start.8 = (s32[12]{0:T(128)S(1)}, s32[12]{0:T(128)}, u32[]{:S(2)}) copy-start(s32[12]{0:T(128)} %copy-done.6) | copy-start | bytes 148
  61.8 12.1 %collective-permute-start.16 = (bf16[12,112,256]{2,1,0:T(8,128)(2,1)S(1)}, bf16[12,112,256]{2,1,0:T(8,128)(2,1)S(1)}, u32[]{:S(2)}, u32[]{:S(2)}) collective-permute-start(bf16[12,112,256]{2,1,0:T(8,128)(2,1)S(1)} %collective-permute-done.9.refs_1_), channel_id=1, source_target_pairs={{0,2},{1,7},{2,4},{3,1},{4,6},{5,3},{6,0},{7,5},{8,10},{9,15},{10,... | collective-permute-start | bytes 2064392 | tf_op jit(solution)/shard_map/ppermute | solution.py:255
  64.9 27.2 %all-to-all-start.1 = ((s16[16,176,256]{2,1,0:T(8,128)(2,1)}), s16[16,176,256]{2,1,0:T(8,128)(2,1)}, u32[]{:S(2)}, u32[]{:S(2)}) async-start(s16[16,176,256]{2,1,0:T(8,128)(2,1)} %get-tuple-element.39), calls=%async_computation.1 | async-start | bytes 2883584 | tf_op jit(solution)/shard_map/all_to_all | solution.py:297
  69.3 5.2 %collective-permute-start.19 = (bf16[12,112,256]{2,1,0:T(8,128)(2,1)S(1)}, bf16[12,112,256]{2,1,0:T(8,128)(2,1)S(1)}, u32[]{:S(2)}, u32[]{:S(2)}) collective-permute-start(bf16[12,112,256]{2,1,0:T(8,128)(2,1)S(1)} %collective-permute-done.15.refs_2_), channel_id=1, source_target_pairs={{0,1},{1,0},{2,3},{3,2},{4,5},{5,4},{6,7},{7,6},{8,9},{9,8},{10,11... | collective-permute-start | bytes 2064392 | tf_op jit(solution)/shard_map/ppermute | solution.py:255
  69.4 5.1 %collective-permute-start.18 = (bf16[12,112,256]{2,1,0:T(8,128)(2,1)S(1)}, bf16[12,112,256]{2,1,0:T(8,128)(2,1)S(1)}, u32[]{:S(2)}, u32[]{:S(2)}) collective-permute-start(bf16[12,112,256]{2,1,0:T(8,128)(2,1)S(1)} %collective-permute-done.9.refs_1_), channel_id=1, source_target_pairs={{0,1},{1,0},{2,3},{3,2},{4,5},{5,4},{6,7},{7,6},{8,9},{9,8},{10,11... | collective-permute-start | bytes 2064392 | tf_op jit(solution)/shard_map/ppermute | solution.py:255
  73.9 2.1 %collective-permute-start.17 = (bf16[12,112,256]{2,1,0:T(8,128)(2,1)S(1)}, bf16[12,112,256]{2,1,0:T(8,128)(2,1)S(1)}, u32[]{:S(2)}, u32[]{:S(2)}) collective-permute-start(bf16[12,112,256]{2,1,0:T(8,128)(2,1)S(1)} %shard_map.65.refs_0_), channel_id=1, source_target_pairs={{0,1},{1,0},{2,3},{3,2},{4,5},{5,4},{6,7},{7,6},{8,9},{9,8},{10,11... | collective-permute-start | bytes 2064392 | tf_op jit(solution)/shard_map/ppermute | solution.py:255
  73.9 3.1 %collective-permute-start.20 = (bf16[12,112,256]{2,1,0:T(8,128)(2,1)S(1)}, bf16[12,112,256]{2,1,0:T(8,128)(2,1)S(1)}, u32[]{:S(2)}, u32[]{:S(2)}) collective-permute-start(bf16[12,112,256]{2,1,0:T(8,128)(2,1)S(1)} %collective-permute-done.16.refs_3_), channel_id=1, source_target_pairs={{0,1},{1,0},{2,3},{3,2},{4,5},{5,4},{6,7},{7,6},{8,9},{9,8},{10,11... | collective-permute-start | bytes 2064392 | tf_op jit(solution)/shard_map/ppermute | solution.py:255
  92.0 33.0 %all-to-all-start = ((s16[16,240,256]{2,1,0:T(8,128)(2,1)}), s16[16,240,256]{2,1,0:T(8,128)(2,1)S(1)}, u32[]{:S(2)}, u32[]{:S(2)}) async-start(s16[16,240,256]{2,1,0:T(8,128)(2,1)} %get-tuple-element.38), calls=%async_computation | async-start | bytes 3932160 | tf_op jit(solution)/shard_map/all_to_all | solution.py:297
